TPU v7x, 512 devices: a whole 4x4x16 slice. The times are simulated.
512 devices in a mesh: blk: 128 (over y_lo, x, z), pair: 4 (over y_hi, core).
Axes of the slice: x: 4, y: 4 (y_hi: 2, y_lo: 2; y = y_hi * 2 + y_lo), z: 16, core: 2. Of those that a mesh axis runs over, the one named last changes fastest.
Arguments:
- points: bfloat16 [16, 1048576], P(None, ('blk', 'pair')), may hold values from -6 to 6
- values: bfloat16 [8, 1048576], P(None, ('blk', 'pair')), may hold values from -0.5 to 0.5
- length_scales: float32 [16], replicated, may hold values from 1.5 to 6
- partners: int32 [2, 128], P(None, 'blk'), may hold values from 0 to 127, as said below
Outputs:
- product: float32 [8, 1048576], P(None, ('blk', 'pair'))
Inputs may be any that keep to these rules, and one draw needn't show every extreme that they name: In round r every block b is paired with b XOR m_r, where m_r is a nonzero mask shared by all blocks of that round and different from the other rounds' masks; so partners[r, partners[r, b]] = b.
All inputs are finite; a program needn't handle non-finite values.
Results may differ from a plain program's by a relative error of at most 0.003.
Values may be sent and summed in bfloat16 or wider, within the bound.
No kernel may reach another device: no remote copies, remote signals or barrier semaphores. Data moves between devices by JAX's collectives and lax.ppermute only.
A program may use at most 64 MiB of HBM per device.

v0:
```python
import jax
import jax.numpy as jnp
from jax import lax
from jax.sharding import PartitionSpec as P


def from_partner(shard, axis, stride):
    return lax.ppermute(shard, axis, [(i, i ^ 1 << stride) for i in range(lax.axis_size(axis))])


def pick_rounds(round_masks, bit_number, moved, kept):
    take_bit = jnp.bitwise_and(jnp.right_shift(round_masks, bit_number), 1) == 1
    take_shape = (take_bit.shape[0],) + (1,) * (kept.ndim - 1)
    return jnp.where(take_bit.reshape(take_shape), moved, kept)


def fetch_apart(far_pts, far_vals, round_masks, bit_count):
    for bit_number in range(bit_count):
        moved_pts, moved_vals = from_partner((far_pts, far_vals), "blk", bit_number)
        far_pts = pick_rounds(round_masks, bit_number, moved_pts, far_pts)
        far_vals = pick_rounds(round_masks, bit_number, moved_vals, far_vals)
    return (far_pts, far_vals)


def return_apart(far_terms, round_masks, bit_count):
    for bit_number in range(bit_count):
        moved_terms = from_partner(far_terms, "blk", bit_number)
        far_terms = pick_rounds(round_masks, bit_number, moved_terms, far_terms)
    return far_terms


def scale_points(raw_points, length_scales):
    scaled = raw_points.astype(jnp.float32) / length_scales[:, None]
    return (scaled, jnp.sum(scaled * scaled, axis=0))


def serve_pairing(own_scaled, own_sq, own_vals, far_scaled, far_sq, far_vals):
    row_count = own_scaled.shape[1]
    col_count = far_scaled.shape[1]
    rhs_count = own_vals.shape[0]
    block_step = min(512, row_count)

    def row_step(row_index, row_carry):
        near_out, far_terms = row_carry
        row_scaled = lax.dynamic_slice_in_dim(own_scaled, row_index * block_step, block_step, 1)
        row_sq = lax.dynamic_slice_in_dim(own_sq, row_index * block_step, block_step, 0)
        row_vals = lax.dynamic_slice_in_dim(own_vals, row_index * block_step, block_step, 1)

        def col_step(col_index, col_carry):
            near_total, inner_terms = col_carry
            col_scaled = lax.dynamic_slice_in_dim(far_scaled, col_index * block_step, block_step, 1)
            col_sq = lax.dynamic_slice_in_dim(far_sq, col_index * block_step, block_step, 0)
            col_vals = lax.dynamic_slice_in_dim(far_vals, col_index * block_step, block_step, 1)
            cross_dot = lax.dot_general(
                row_scaled,
                col_scaled,
                (((0,), (0,)), ((), ())),
                precision=lax.Precision.HIGHEST,
                preferred_element_type=jnp.float32,
            )
            kernel = jnp.exp(-0.5 * (row_sq[:, None] + col_sq[None, :] - 2.0 * cross_dot)).astype(
                jnp.bfloat16
            )
            near_total = near_total + lax.dot_general(
                col_vals, kernel, (((1,), (1,)), ((), ())), preferred_element_type=jnp.float32
            )
            tile_piece = jnp.dot(row_vals, kernel, preferred_element_type=jnp.float32)
            prior_terms = lax.dynamic_slice_in_dim(
                inner_terms, col_index * block_step, block_step, 1
            )
            inner_terms = lax.dynamic_update_slice_in_dim(
                inner_terms, prior_terms + tile_piece, col_index * block_step, 1
            )
            return (near_total, inner_terms)

        near_total, far_terms = lax.fori_loop(
            0,
            col_count // block_step,
            col_step,
            (jnp.zeros((rhs_count, block_step), jnp.float32), far_terms),
        )
        near_out = lax.dynamic_update_slice_in_dim(near_out, near_total, row_index * block_step, 1)
        return (near_out, far_terms)

    start_carry = (
        jnp.zeros((rhs_count, row_count), jnp.float32),
        jnp.zeros((rhs_count, col_count), jnp.float32),
    )
    return lax.fori_loop(0, row_count // block_step, row_step, start_carry)


def shards(points, values, length_scales, partners):
    rounds = partners.shape[0]
    local_count = points.shape[1]
    rhs_count = values.shape[0]
    groups = lax.axis_size("pair")
    half_groups = groups // 2
    bit_count = lax.axis_size("blk").bit_length() - 1
    own_block = lax.axis_index("blk")
    own_quarter = lax.axis_index("pair")
    partner_ids = partners[:, 0]
    round_masks = jnp.bitwise_xor(partner_ids, own_block)
    is_lower = own_block < partner_ids
    own_scaled, own_sq = scale_points(points, length_scales)
    send_pts = jnp.broadcast_to(points[None], (rounds,) + points.shape)
    send_vals = jnp.broadcast_to(values[None], (rounds,) + values.shape)
    fetched = [
        fetch_apart(
            send_pts[round_index : round_index + 1],
            send_vals[round_index : round_index + 1],
            round_masks[round_index : round_index + 1],
            bit_count,
        )
        for round_index in range(rounds)
    ]
    far_pts = jnp.concatenate([result_pair[0] for result_pair in fetched], 0)
    far_vals = jnp.concatenate([result_pair[1] for result_pair in fetched], 0)
    near_sum = jnp.zeros((rhs_count, local_count), jnp.float32)
    term_list = []
    for round_index in range(rounds):
        whole_pts, whole_vals = (
            lax.all_gather(far_pts[round_index], "pair", axis=1, tiled=True),
            lax.all_gather(far_vals[round_index], "pair", axis=1, tiled=True),
        )
        base_own = jnp.where(is_lower[round_index], 0, 1)
        chosen_pts = []
        chosen_vals = []
        for slot_index in range(half_groups):
            first_col = (own_quarter + base_own + slot_index) % groups * local_count
            chosen_pts.append(lax.dynamic_slice_in_dim(whole_pts, first_col, local_count, 1))
            chosen_vals.append(lax.dynamic_slice_in_dim(whole_vals, first_col, local_count, 1))
        far_scaled, far_sq = scale_points(jnp.concatenate(chosen_pts, 1), length_scales)
        near_part, far_part = serve_pairing(
            own_scaled, own_sq, values, far_scaled, far_sq, jnp.concatenate(chosen_vals, 1)
        )
        near_sum = near_sum + near_part
        term_list.append(far_part.reshape(rhs_count, half_groups, local_count))
    far_terms = jnp.stack(term_list)
    back_terms = jnp.concatenate(
        [
            return_apart(
                far_terms[round_index : round_index + 1],
                round_masks[round_index : round_index + 1],
                bit_count,
            )
            for round_index in range(rounds)
        ],
        0,
    )
    incoming_sum = jnp.zeros((rhs_count, local_count), jnp.float32)
    for round_index in range(rounds):
        sender_base = jnp.where(is_lower[round_index], 1, 0)
        dest_quarter = (
            own_quarter + sender_base + jnp.arange(half_groups, dtype=jnp.int32)
        ) % groups
        onehot = (dest_quarter[:, None] == jnp.arange(groups, dtype=jnp.int32)[None, :]).astype(
            jnp.float32
        )
        spread = jnp.einsum(
            "tg,rtq->grq", onehot, back_terms[round_index], precision=lax.Precision.HIGHEST
        )
        incoming_sum = (
            incoming_sum + lax.psum_scatter(spread, "pair", scatter_dimension=0, tiled=True)[0]
        )
    return near_sum + incoming_sum


def solution(mesh):
    placed = (P(None, ("blk", "pair")), P(None, ("blk", "pair")), P(), P(None, "blk"))
    return jax.shard_map(
        shards, mesh=mesh, in_specs=placed, out_specs=P(None, ("blk", "pair")), check_vma=False
    )
```

profile of v0, /device:TPU:1, one launch (start us, length us, event | category | flops | bytes accessed | tf_op | source)
XLA Modules:
  0.0 425.9 jit_solution(7658868877562527371)
XLA Ops:
  6.5 4.4 %collective-permute-start = (bf16[1,8,2048]{2,1,0:T(8,128)(2,1)}, bf16[1,8,2048]{2,1,0:T(8,128)(2,1)S(1)}, u32[]{:S(2)}, u32[]{:S(2)}) collective-permute-start(bf16[1,8,2048]{2,1,0:T(8,128)(2,1)} %bitcast.166), channel_id=1, source_target_pairs={{0,4},{4,0},{8,12},{12,8},{16,20},{20,16},{24,28},{28,24},{32,36},... | collective-permute-start | bytes 98312 | tf_op jit(solution)/shard_map/ppermute | solution.py:8
  18.8 4.9 %collective-permute-start.14 = (bf16[1,8,2048]{2,1,0:T(8,128)(2,1)S(1)}, bf16[1,8,2048]{2,1,0:T(8,128)(2,1)S(1)}, u32[]{:S(2)}, u32[]{:S(2)}) collective-permute-start(bf16[1,8,2048]{2,1,0:T(8,128)(2,1)S(1)} %get-tuple-element.826), channel_id=1, source_target_pairs={{0,8},{4,12},{8,0},{12,4},{16,24},{20,28},{24,16},{28,20},{32,40},... | collective-permute-start | bytes 98312 | tf_op jit(solution)/shard_map/ppermute | solution.py:8
  34.1 8.8 %collective-permute-start.15 = (bf16[1,8,2048]{2,1,0:T(8,128)(2,1)S(1)}, bf16[1,8,2048]{2,1,0:T(8,128)(2,1)S(1)}, u32[]{:S(2)}, u32[]{:S(2)}) collective-permute-start(bf16[1,8,2048]{2,1,0:T(8,128)(2,1)S(1)} %broadcast_select_fusion.27), channel_id=1, source_target_pairs={{0,16},{4,20},{8,24},{12,28},{16,0},{20,4},{24,8},{28,12},{32,48},... | collective-permute-start | bytes 98312 | tf_op jit(solution)/shard_map/ppermute | solution.py:8
  43.0 4.3 %collective-permute-start.8 = (bf16[1,16,2048]{2,1,0:T(8,128)(2,1)S(1)}, bf16[1,16,2048]{2,1,0:T(8,128)(2,1)S(1)}, u32[]{:S(2)}, u32[]{:S(2)}) collective-permute-start(bf16[1,16,2048]{2,1,0:T(8,128)(2,1)S(1)} %get-tuple-element.819), channel_id=1, source_target_pairs={{0,8},{4,12},{8,0},{12,4},{16,24},{20,28},{24,16},{28,20},{32,40},... | collective-permute-start | bytes 196616 | tf_op jit(solution)/shard_map/ppermute | solution.py:8
  51.2 13.1 %collective-permute-start.16 = (bf16[1,8,2048]{2,1,0:T(8,128)(2,1)S(1)}, bf16[1,8,2048]{2,1,0:T(8,128)(2,1)S(1)}, u32[]{:S(2)}, u32[]{:S(2)}) collective-permute-start(bf16[1,8,2048]{2,1,0:T(8,128)(2,1)S(1)} %broadcast_select_fusion.28), channel_id=1, source_target_pairs={{0,32},{4,36},{8,40},{12,44},{16,48},{20,52},{24,56},{28,60},{32,0... | collective-permute-start | bytes 98312 | tf_op jit(solution)/shard_map/ppermute | solution.py:8
  64.3 3.3 collective-permute-start.3
  67.6 3.1 collective-permute-start.17
  70.8 5.9 %collective-permute-start.9 = (bf16[1,16,2048]{2,1,0:T(8,128)(2,1)S(1)}, bf16[1,16,2048]{2,1,0:T(8,128)(2,1)S(1)}, u32[]{:S(2)}, u32[]{:S(2)}) collective-permute-start(bf16[1,16,2048]{2,1,0:T(8,128)(2,1)S(1)} %broadcast_select_fusion.20), channel_id=1, source_target_pairs={{0,16},{4,20},{8,24},{12,28},{16,0},{20,4},{24,8},{28,12},{32,48},... | collective-permute-start | bytes 196616 | tf_op jit(solution)/shard_map/ppermute | solution.py:8
  76.7 3.3 collective-permute-start.21
  82.2 4.7 %collective-permute-start.18 = (bf16[1,8,2048]{2,1,0:T(8,128)(2,1)S(1)}, bf16[1,8,2048]{2,1,0:T(8,128)(2,1)S(1)}, u32[]{:S(2)}, u32[]{:S(2)}) collective-permute-start(bf16[1,8,2048]{2,1,0:T(8,128)(2,1)S(1)} %broadcast_select_fusion.30), channel_id=1, source_target_pairs={{0,128},{4,132},{8,136},{12,140},{16,144},{20,148},{24,152},{28,15... | collective-permute-start | bytes 98312 | tf_op jit(solution)/shard_map/ppermute | solution.py:8
  89.4 10.7 %collective-permute-start.10 = (bf16[1,16,2048]{2,1,0:T(8,128)(2,1)S(1)}, bf16[1,16,2048]{2,1,0:T(8,128)(2,1)S(1)}, u32[]{:S(2)}, u32[]{:S(2)}) collective-permute-start(bf16[1,16,2048]{2,1,0:T(8,128)(2,1)S(1)} %broadcast_select_fusion.21), channel_id=1, source_target_pairs={{0,32},{4,36},{8,40},{12,44},{16,48},{20,52},{24,56},{28,60},{32,0... | collective-permute-start | bytes 196616 | tf_op jit(solution)/shard_map/ppermute | solution.py:8
  100.1 3.3 collective-permute-start.22
  103.5 3.2 collective-permute-start.19
  108.8 13.9 %all-gather.2 = bf16[1,8,8192]{2,1,0:T(8,128)(2,1)S(1)} all-gather(bf16[1,8,2048]{2,1,0:T(8,128)(2,1)S(1)} %broadcast_select_fusion.32), channel_id=4, replica_groups=mesh['blk'=128,'pair'=4] {'pair'}, dimensions={2}, use_global_device_ids=true | all-gather | bytes 163840 | tf_op jit(solution)/shard_map/all_gather | solution.py:123
  122.8 6.9 %all-gather = bf16[1,8,8192]{2,1,0:T(8,128)(2,1)S(1)} all-gather(bf16[1,8,2048]{2,1,0:T(8,128)(2,1)S(1)} %broadcast_select_fusion.39), channel_id=2, replica_groups=mesh['blk'=128,'pair'=4] {'pair'}, dimensions={2}, use_global_device_ids=true | all-gather | bytes 163840 | tf_op jit(solution)/shard_map/all_gather | solution.py:123
  129.8 2.5 collective-permute-start.11
  132.3 2.8 collective-permute-start.23
  135.2 4.1 collective-permute-start.12
  139.3 2.7 collective-permute-start.24
  142.1 3.2 collective-permute-start.13
  145.8 3.2 collective-permute-start.25
  149.1 9.8 %all-gather.1 = bf16[1,16,8192]{2,1,0:T(8,128)(2,1)S(1)} all-gather(bf16[1,16,2048]{2,1,0:T(8,128)(2,1)S(1)} %broadcast_select_fusion.25), channel_id=3, replica_groups=mesh['blk'=128,'pair'=4] {'pair'}, dimensions={2}, use_global_device_ids=true | all-gather | bytes 327680 | tf_op jit(solution)/shard_map/all_gather | solution.py:122
  159.0 7.4 %all-gather.3 = bf16[1,16,8192]{2,1,0:T(8,128)(2,1)S(1)} all-gather(bf16[1,16,2048]{2,1,0:T(8,128)(2,1)S(1)} %broadcast_select_fusion.18), channel_id=5, replica_groups=mesh['blk'=128,'pair'=4] {'pair'}, dimensions={2}, use_global_device_ids=true | all-gather | bytes 327680 | tf_op jit(solution)/shard_map/all_gather | solution.py:122
  166.6 55.1 %while.93 = (s32[]{:T(128)}, f32[8,2048]{1,0:T(8,128)S(1)}, f32[8,4096]{1,0:T(8,128)S(1)}, f32[16,2048]{1,0:T(8,128)S(1)}, f32[2048]{0:T(1024)S(1)}, /*index=5*/...) while((s32[]{:T(128)}, f32[8,2048]{1,0:T(8,128)S(1)}, ...), condition=%wide.region_10.11_spmd, body=%wide.region_7.10_spmd.sunk | while | flops 60043272 | bytes 1847840 | solution.py:89
  166.7 13.7 %while.95 = (s32[]{:T(128)}, f32[8,512]{1,0:T(8,128)S(1)}, f32[8,4096]{1,0:T(8,128)S(1)}, bf16[8,4096]{1,0:T(8,128)(2,1)S(1)}, f32[512]{0:T(512)S(1)}, /*index=5...) while((s32[]{:T(128)}, f32[8,512]{1,0:T(8,128)S(1)}, ...), condition=%wide.region_9.9_spmd.clone, body=%wide.region_8.8_spmd.clone.sunk | while | flops 60043268 | bytes 1728717 | solution.py:76
  180.5 13.7 %while.95 = (s32[]{:T(128)}, f32[8,512]{1,0:T(8,128)S(1)}, f32[8,4096]{1,0:T(8,128)S(1)}, bf16[8,4096]{1,0:T(8,128)(2,1)S(1)}, f32[512]{0:T(512)S(1)}, /*index=5...) while((s32[]{:T(128)}, f32[8,512]{1,0:T(8,128)S(1)}, ...), condition=%wide.region_9.9_spmd.clone, body=%wide.region_8.8_spmd.clone.sunk | while | flops 60043268 | bytes 1728717 | solution.py:76
  194.2 13.7 %while.95 = (s32[]{:T(128)}, f32[8,512]{1,0:T(8,128)S(1)}, f32[8,4096]{1,0:T(8,128)S(1)}, bf16[8,4096]{1,0:T(8,128)(2,1)S(1)}, f32[512]{0:T(512)S(1)}, /*index=5...) while((s32[]{:T(128)}, f32[8,512]{1,0:T(8,128)S(1)}, ...), condition=%wide.region_9.9_spmd.clone, body=%wide.region_8.8_spmd.clone.sunk | while | flops 60043268 | bytes 1728717 | solution.py:76
  208.0 13.7 %while.95 = (s32[]{:T(128)}, f32[8,512]{1,0:T(8,128)S(1)}, f32[8,4096]{1,0:T(8,128)S(1)}, bf16[8,4096]{1,0:T(8,128)(2,1)S(1)}, f32[512]{0:T(512)S(1)}, /*index=5...) while((s32[]{:T(128)}, f32[8,512]{1,0:T(8,128)S(1)}, ...), condition=%wide.region_9.9_spmd.clone, body=%wide.region_8.8_spmd.clone.sunk | while | flops 60043268 | bytes 1728717 | solution.py:76
  221.8 2.6 collective-permute-start.33
  224.5 55.1 %while.91 = (s32[]{:T(128)}, f32[8,2048]{1,0:T(8,128)S(1)}, f32[8,4096]{1,0:T(8,128)S(1)}, f32[16,2048]{1,0:T(8,128)S(1)}, f32[2048]{0:T(1024)S(1)}, /*index=5*/...) while((s32[]{:T(128)}, f32[8,2048]{1,0:T(8,128)S(1)}, ...), condition=%wide.region_5.6_spmd, body=%wide.region_2.5_spmd.sunk | while | flops 60043272 | bytes 1847840 | solution.py:89
  224.6 13.7 %while.94 = (s32[]{:T(128)}, f32[8,512]{1,0:T(8,128)S(1)}, f32[8,4096]{1,0:T(8,128)S(1)}, bf16[8,4096]{1,0:T(8,128)(2,1)S(1)}, f32[512]{0:T(512)S(1)}, /*index=5...) while((s32[]{:T(128)}, f32[8,512]{1,0:T(8,128)S(1)}, ...), condition=%wide.region_4.4_spmd.clone, body=%wide.region_3.3_spmd.clone.sunk | while | flops 60043268 | bytes 1728717 | solution.py:76
  238.3 13.7 %while.94 = (s32[]{:T(128)}, f32[8,512]{1,0:T(8,128)S(1)}, f32[8,4096]{1,0:T(8,128)S(1)}, bf16[8,4096]{1,0:T(8,128)(2,1)S(1)}, f32[512]{0:T(512)S(1)}, /*index=5...) while((s32[]{:T(128)}, f32[8,512]{1,0:T(8,128)S(1)}, ...), condition=%wide.region_4.4_spmd.clone, body=%wide.region_3.3_spmd.clone.sunk | while | flops 60043268 | bytes 1728717 | solution.py:76
  252.1 13.7 %while.94 = (s32[]{:T(128)}, f32[8,512]{1,0:T(8,128)S(1)}, f32[8,4096]{1,0:T(8,128)S(1)}, bf16[8,4096]{1,0:T(8,128)(2,1)S(1)}, f32[512]{0:T(512)S(1)}, /*index=5...) while((s32[]{:T(128)}, f32[8,512]{1,0:T(8,128)S(1)}, ...), condition=%wide.region_4.4_spmd.clone, body=%wide.region_3.3_spmd.clone.sunk | while | flops 60043268 | bytes 1728717 | solution.py:76
  265.9 13.7 %while.94 = (s32[]{:T(128)}, f32[8,512]{1,0:T(8,128)S(1)}, f32[8,4096]{1,0:T(8,128)S(1)}, bf16[8,4096]{1,0:T(8,128)(2,1)S(1)}, f32[512]{0:T(512)S(1)}, /*index=5...) while((s32[]{:T(128)}, f32[8,512]{1,0:T(8,128)S(1)}, ...), condition=%wide.region_4.4_spmd.clone, body=%wide.region_3.3_spmd.clone.sunk | while | flops 60043268 | bytes 1728717 | solution.py:76
  279.6 2.6 collective-permute-start.26
  282.4 3.1 collective-permute-start.34
  286.3 3.1 collective-permute-start.27
  289.4 6.4 %collective-permute-done.34 = f32[1,8,2,2048]{3,2,1,0:T(2,128)S(1)} collective-permute-done((f32[1,8,2,2048]{3,2,1,0:T(2,128)S(1)}, f32[1,8,2,2048]{3,2,1,0:T(2,128)S(1)}, u32[]{:S(2)}, u32[]{:S(2)}) %collective-permute-start.34) | collective-permute-done | bytes 131104 | tf_op jit(solution)/shard_map/ppermute | solution.py:8
  298.6 6.4 %collective-permute-start.28 = (f32[1,8,2,2048]{3,2,1,0:T(2,128)S(1)}, f32[1,8,2,2048]{3,2,1,0:T(2,128)S(1)}, u32[]{:S(2)}, u32[]{:S(2)}) collective-permute-start(f32[1,8,2,2048]{3,2,1,0:T(2,128)S(1)} %bitcast.157), channel_id=1, source_target_pairs={{0,16},{4,20},{8,24},{12,28},{16,0},{20,4},{24,8},{28,12},{32,48},... | collective-permute-start | bytes 393224 | tf_op jit(solution)/shard_map/ppermute | solution.py:8
  305.0 18.7 %collective-permute-done.35 = f32[1,8,2,2048]{3,2,1,0:T(2,128)S(1)} collective-permute-done((f32[1,8,2,2048]{3,2,1,0:T(2,128)S(1)}, f32[1,8,2,2048]{3,2,1,0:T(2,128)S(1)}, u32[]{:S(2)}, u32[]{:S(2)}) %collective-permute-start.35) | collective-permute-done | bytes 131104 | tf_op jit(solution)/shard_map/ppermute | solution.py:8
  323.7 8.8 %collective-permute-start.36 = (f32[1,8,2,2048]{3,2,1,0:T(2,128)S(1)}, f32[1,8,2,2048]{3,2,1,0:T(2,128)S(1)}, u32[]{:S(2)}, u32[]{:S(2)}) collective-permute-start(f32[1,8,2,2048]{3,2,1,0:T(2,128)S(1)} %bitcast.158), channel_id=1, source_target_pairs={{0,32},{4,36},{8,40},{12,44},{16,48},{20,52},{24,56},{28,60},{32,0... | collective-permute-start | bytes 393224 | tf_op jit(solution)/shard_map/ppermute | solution.py:8
  332.6 5.6 %collective-permute-start.29 = (f32[1,8,2,2048]{3,2,1,0:T(2,128)S(1)}, f32[1,8,2,2048]{3,2,1,0:T(2,128)S(1)}, u32[]{:S(2)}, u32[]{:S(2)}) collective-permute-start(f32[1,8,2,2048]{3,2,1,0:T(2,128)S(1)} %bitcast.159), channel_id=1, source_target_pairs={{0,32},{4,36},{8,40},{12,44},{16,48},{20,52},{24,56},{28,60},{32,0... | collective-permute-start | bytes 393224 | tf_op jit(solution)/shard_map/ppermute | solution.py:8
  338.2 13.9 %collective-permute-done.36 = f32[1,8,2,2048]{3,2,1,0:T(2,128)S(1)} collective-permute-done((f32[1,8,2,2048]{3,2,1,0:T(2,128)S(1)}, f32[1,8,2,2048]{3,2,1,0:T(2,128)S(1)}, u32[]{:S(2)}, u32[]{:S(2)}) %collective-permute-start.36) | collective-permute-done | bytes 131104 | tf_op jit(solution)/shard_map/ppermute | solution.py:8
  358.5 2.8 collective-permute-start.38
  361.4 3.9 collective-permute-start.31
  369.1 2.7 collective-permute-start.32
  372.3 4.0 collective-permute-done.32
  377.7 39.9 %reduce-scatter.2.cloned.1.call-done = f32[1,8,2048]{2,1,0:T(8,128)} async-done(((f32[4,8,2048]{2,1,0:T(8,128)}), f32[1,8,2048]{2,1,0:T(8,128)}) %reduce-scatter.2.cloned.1.call-update) | async-done | bytes 65552 | tf_op jit(solution)/shard_map/reduce_scatter | solution.py:163
  (415 shorter events, 145.7 us)
Async XLA Ops:
  6.5 411.1 %reduce-scatter.2.cloned.1.call-start = ((), (), s32[]{:S(2)}) async-start(), calls=%async_computation.1 | async-start | bytes 327680 | tf_op jit(solution)/shard_map/reduce_scatter | solution.py:163
  6.5 12.2 %collective-permute-start = (bf16[1,8,2048]{2,1,0:T(8,128)(2,1)}, bf16[1,8,2048]{2,1,0:T(8,128)(2,1)S(1)}, u32[]{:S(2)}, u32[]{:S(2)}) collective-permute-start(bf16[1,8,2048]{2,1,0:T(8,128)(2,1)} %bitcast.166), channel_id=1, source_target_pairs={{0,4},{4,0},{8,12},{12,8},{16,20},{20,16},{24,28},{28,24},{32,36},... | collective-permute-start | bytes 98312 | tf_op jit(solution)/shard_map/ppermute | solution.py:8
  10.9 32.0 %collective-permute-start.7 = (bf16[1,16,2048]{2,1,0:T(8,128)(2,1)}, bf16[1,16,2048]{2,1,0:T(8,128)(2,1)S(1)}, u32[]{:S(2)}, u32[]{:S(2)}) collective-permute-start(bf16[1,16,2048]{2,1,0:T(8,128)(2,1)} %bitcast.167), channel_id=1, source_target_pairs={{0,4},{4,0},{8,12},{12,8},{16,20},{20,16},{24,28},{28,24},{32,36},... | collective-permute-start | bytes 196616 | tf_op jit(solution)/shard_map/ppermute | solution.py:8
  12.8 0.7 copy-start.3
  13.5 0.7 copy-start.2
  15.1 3.7 copy-start
  18.8 15.3 %collective-permute-start.14 = (bf16[1,8,2048]{2,1,0:T(8,128)(2,1)S(1)}, bf16[1,8,2048]{2,1,0:T(8,128)(2,1)S(1)}, u32[]{:S(2)}, u32[]{:S(2)}) collective-permute-start(bf16[1,8,2048]{2,1,0:T(8,128)(2,1)S(1)} %get-tuple-element.826), channel_id=1, source_target_pairs={{0,8},{4,12},{8,0},{12,4},{16,24},{20,28},{24,16},{28,20},{32,40},... | collective-permute-start | bytes 98312 | tf_op jit(solution)/shard_map/ppermute | solution.py:8
  32.1 10.8 %copy-start.1 = (bf16[16,2048]{1,0:T(8,128)(2,1)S(1)}, bf16[16,2048]{1,0:T(8,128)(2,1)}, u32[]{:S(2)}) copy-start(bf16[16,2048]{1,0:T(8,128)(2,1)} %param.12) | copy-start | bytes 196612
  32.2 17.0 %collective-permute-start.1 = (bf16[1,8,2048]{2,1,0:T(8,128)(2,1)S(1)}, bf16[1,8,2048]{2,1,0:T(8,128)(2,1)S(1)}, u32[]{:S(2)}, u32[]{:S(2)}) collective-permute-start(bf16[1,8,2048]{2,1,0:T(8,128)(2,1)S(1)} %get-tuple-element.825), channel_id=1, source_target_pairs={{0,8},{4,12},{8,0},{12,4},{16,24},{20,28},{24,16},{28,20},{32,40},... | collective-permute-start | bytes 98312 | tf_op jit(solution)/shard_map/ppermute | solution.py:8
  34.1 17.0 %collective-permute-start.15 = (bf16[1,8,2048]{2,1,0:T(8,128)(2,1)S(1)}, bf16[1,8,2048]{2,1,0:T(8,128)(2,1)S(1)}, u32[]{:S(2)}, u32[]{:S(2)}) collective-permute-start(bf16[1,8,2048]{2,1,0:T(8,128)(2,1)S(1)} %broadcast_select_fusion.27), channel_id=1, source_target_pairs={{0,16},{4,20},{8,24},{12,28},{16,0},{20,4},{24,8},{28,12},{32,48},... | collective-permute-start | bytes 98312 | tf_op jit(solution)/shard_map/ppermute | solution.py:8
  43.0 27.8 %collective-permute-start.8 = (bf16[1,16,2048]{2,1,0:T(8,128)(2,1)S(1)}, bf16[1,16,2048]{2,1,0:T(8,128)(2,1)S(1)}, u32[]{:S(2)}, u32[]{:S(2)}) collective-permute-start(bf16[1,16,2048]{2,1,0:T(8,128)(2,1)S(1)} %get-tuple-element.819), channel_id=1, source_target_pairs={{0,8},{4,12},{8,0},{12,4},{16,24},{20,28},{24,16},{28,20},{32,40},... | collective-permute-start | bytes 196616 | tf_op jit(solution)/shard_map/ppermute | solution.py:8
  47.3 29.4 %collective-permute-start.20 = (bf16[1,16,2048]{2,1,0:T(8,128)(2,1)S(1)}, bf16[1,16,2048]{2,1,0:T(8,128)(2,1)S(1)}, u32[]{:S(2)}, u32[]{:S(2)}) collective-permute-start(bf16[1,16,2048]{2,1,0:T(8,128)(2,1)S(1)} %get-tuple-element.820), channel_id=1, source_target_pairs={{0,8},{4,12},{8,0},{12,4},{16,24},{20,28},{24,16},{28,20},{32,40},... | collective-permute-start | bytes 196616 | tf_op jit(solution)/shard_map/ppermute | solution.py:8
  49.2 15.0 %collective-permute-start.2 = (bf16[1,8,2048]{2,1,0:T(8,128)(2,1)S(1)}, bf16[1,8,2048]{2,1,0:T(8,128)(2,1)S(1)}, u32[]{:S(2)}, u32[]{:S(2)}) collective-permute-start(bf16[1,8,2048]{2,1,0:T(8,128)(2,1)S(1)} %broadcast_select_fusion.34), channel_id=1, source_target_pairs={{0,16},{4,20},{8,24},{12,28},{16,0},{20,4},{24,8},{28,12},{32,48},... | collective-permute-start | bytes 98312 | tf_op jit(solution)/shard_map/ppermute | solution.py:8
  51.2 16.4 %collective-permute-start.16 = (bf16[1,8,2048]{2,1,0:T(8,128)(2,1)S(1)}, bf16[1,8,2048]{2,1,0:T(8,128)(2,1)S(1)}, u32[]{:S(2)}, u32[]{:S(2)}) collective-permute-start(bf16[1,8,2048]{2,1,0:T(8,128)(2,1)S(1)} %broadcast_select_fusion.28), channel_id=1, source_target_pairs={{0,32},{4,36},{8,40},{12,44},{16,48},{20,52},{24,56},{28,60},{32,0... | collective-permute-start | bytes 98312 | tf_op jit(solution)/shard_map/ppermute | solution.py:8
  64.3 15.8 %collective-permute-start.3 = (bf16[1,8,2048]{2,1,0:T(8,128)(2,1)S(1)}, bf16[1,8,2048]{2,1,0:T(8,128)(2,1)S(1)}, u32[]{:S(2)}, u32[]{:S(2)}) collective-permute-start(bf16[1,8,2048]{2,1,0:T(8,128)(2,1)S(1)} %broadcast_select_fusion.35), channel_id=1, source_target_pairs={{0,32},{4,36},{8,40},{12,44},{16,48},{20,52},{24,56},{28,60},{32,0... | collective-permute-start | bytes 98312 | tf_op jit(solution)/shard_map/ppermute | solution.py:8
  67.6 14.6 %collective-permute-start.17 = (bf16[1,8,2048]{2,1,0:T(8,128)(2,1)S(1)}, bf16[1,8,2048]{2,1,0:T(8,128)(2,1)S(1)}, u32[]{:S(2)}, u32[]{:S(2)}) collective-permute-start(bf16[1,8,2048]{2,1,0:T(8,128)(2,1)S(1)} %broadcast_select_fusion.29), channel_id=1, source_target_pairs={{0,64},{4,68},{8,72},{12,76},{16,80},{20,84},{24,88},{28,92},{32,9... | collective-permute-start | bytes 98312 | tf_op jit(solution)/shard_map/ppermute | solution.py:8
  70.8 18.6 %collective-permute-start.9 = (bf16[1,16,2048]{2,1,0:T(8,128)(2,1)S(1)}, bf16[1,16,2048]{2,1,0:T(8,128)(2,1)S(1)}, u32[]{:S(2)}, u32[]{:S(2)}) collective-permute-start(bf16[1,16,2048]{2,1,0:T(8,128)(2,1)S(1)} %broadcast_select_fusion.20), channel_id=1, source_target_pairs={{0,16},{4,20},{8,24},{12,28},{16,0},{20,4},{24,8},{28,12},{32,48},... | collective-permute-start | bytes 196616 | tf_op jit(solution)/shard_map/ppermute | solution.py:8
  76.7 23.4 %collective-permute-start.21 = (bf16[1,16,2048]{2,1,0:T(8,128)(2,1)S(1)}, bf16[1,16,2048]{2,1,0:T(8,128)(2,1)S(1)}, u32[]{:S(2)}, u32[]{:S(2)}) collective-permute-start(bf16[1,16,2048]{2,1,0:T(8,128)(2,1)S(1)} %broadcast_select_fusion.13), channel_id=1, source_target_pairs={{0,16},{4,20},{8,24},{12,28},{16,0},{20,4},{24,8},{28,12},{32,48},... | collective-permute-start | bytes 196616 | tf_op jit(solution)/shard_map/ppermute | solution.py:8
  80.0 6.9 %collective-permute-start.4 = (bf16[1,8,2048]{2,1,0:T(8,128)(2,1)S(1)}, bf16[1,8,2048]{2,1,0:T(8,128)(2,1)S(1)}, u32[]{:S(2)}, u32[]{:S(2)}) collective-permute-start(bf16[1,8,2048]{2,1,0:T(8,128)(2,1)S(1)} %broadcast_select_fusion.36), channel_id=1, source_target_pairs={{0,64},{4,68},{8,72},{12,76},{16,80},{20,84},{24,88},{28,92},{32,9... | collective-permute-start | bytes 98312 | tf_op jit(solution)/shard_map/ppermute | solution.py:8
  82.2 21.2 %collective-permute-start.18 = (bf16[1,8,2048]{2,1,0:T(8,128)(2,1)S(1)}, bf16[1,8,2048]{2,1,0:T(8,128)(2,1)S(1)}, u32[]{:S(2)}, u32[]{:S(2)}) collective-permute-start(bf16[1,8,2048]{2,1,0:T(8,128)(2,1)S(1)} %broadcast_select_fusion.30), channel_id=1, source_target_pairs={{0,128},{4,132},{8,136},{12,140},{16,144},{20,148},{24,152},{28,15... | collective-permute-start | bytes 98312 | tf_op jit(solution)/shard_map/ppermute | solution.py:8
  86.9 19.8 %collective-permute-start.5 = (bf16[1,8,2048]{2,1,0:T(8,128)(2,1)S(1)}, bf16[1,8,2048]{2,1,0:T(8,128)(2,1)S(1)}, u32[]{:S(2)}, u32[]{:S(2)}) collective-permute-start(bf16[1,8,2048]{2,1,0:T(8,128)(2,1)S(1)} %broadcast_select_fusion.37), channel_id=1, source_target_pairs={{0,128},{4,132},{8,136},{12,140},{16,144},{20,148},{24,152},{28,15... | collective-permute-start | bytes 98312 | tf_op jit(solution)/shard_map/ppermute | solution.py:8
  89.4 40.3 %collective-permute-start.10 = (bf16[1,16,2048]{2,1,0:T(8,128)(2,1)S(1)}, bf16[1,16,2048]{2,1,0:T(8,128)(2,1)S(1)}, u32[]{:S(2)}, u32[]{:S(2)}) collective-permute-start(bf16[1,16,2048]{2,1,0:T(8,128)(2,1)S(1)} %broadcast_select_fusion.21), channel_id=1, source_target_pairs={{0,32},{4,36},{8,40},{12,44},{16,48},{20,52},{24,56},{28,60},{32,0... | collective-permute-start | bytes 196616 | tf_op jit(solution)/shard_map/ppermute | solution.py:8
  100.1 32.2 %collective-permute-start.22 = (bf16[1,16,2048]{2,1,0:T(8,128)(2,1)S(1)}, bf16[1,16,2048]{2,1,0:T(8,128)(2,1)S(1)}, u32[]{:S(2)}, u32[]{:S(2)}) collective-permute-start(bf16[1,16,2048]{2,1,0:T(8,128)(2,1)S(1)} %broadcast_select_fusion.14), channel_id=1, source_target_pairs={{0,32},{4,36},{8,40},{12,44},{16,48},{20,52},{24,56},{28,60},{32,0... | collective-permute-start | bytes 196616 | tf_op jit(solution)/shard_map/ppermute | solution.py:8
  103.5 5.3 %collective-permute-start.19 = (bf16[1,8,2048]{2,1,0:T(8,128)(2,1)S(1)}, bf16[1,8,2048]{2,1,0:T(8,128)(2,1)S(1)}, u32[]{:S(2)}, u32[]{:S(2)}) collective-permute-start(bf16[1,8,2048]{2,1,0:T(8,128)(2,1)S(1)} %broadcast_select_fusion.31), channel_id=1, source_target_pairs={{0,256},{4,260},{8,264},{12,268},{16,272},{20,276},{24,280},{28,28... | collective-permute-start | bytes 98312 | tf_op jit(solution)/shard_map/ppermute | solution.py:8
  106.7 16.0 %collective-permute-start.6 = (bf16[1,8,2048]{2,1,0:T(8,128)(2,1)S(1)}, bf16[1,8,2048]{2,1,0:T(8,128)(2,1)S(1)}, u32[]{:S(2)}, u32[]{:S(2)}) collective-permute-start(bf16[1,8,2048]{2,1,0:T(8,128)(2,1)S(1)} %broadcast_select_fusion.38), channel_id=1, source_target_pairs={{0,256},{4,260},{8,264},{12,268},{16,272},{20,276},{24,280},{28,28... | collective-permute-start | bytes 98312 | tf_op jit(solution)/shard_map/ppermute | solution.py:8
  129.8 5.4 %collective-permute-start.11 = (bf16[1,16,2048]{2,1,0:T(8,128)(2,1)S(1)}, bf16[1,16,2048]{2,1,0:T(8,128)(2,1)S(1)}, u32[]{:S(2)}, u32[]{:S(2)}) collective-permute-start(bf16[1,16,2048]{2,1,0:T(8,128)(2,1)S(1)} %broadcast_select_fusion.22), channel_id=1, source_target_pairs={{0,64},{4,68},{8,72},{12,76},{16,80},{20,84},{24,88},{28,92},{32,9... | collective-permute-start | bytes 196616 | tf_op jit(solution)/shard_map/ppermute | solution.py:8
  132.3 7.0 %collective-permute-start.23 = (bf16[1,16,2048]{2,1,0:T(8,128)(2,1)S(1)}, bf16[1,16,2048]{2,1,0:T(8,128)(2,1)S(1)}, u32[]{:S(2)}, u32[]{:S(2)}) collective-permute-start(bf16[1,16,2048]{2,1,0:T(8,128)(2,1)S(1)} %broadcast_select_fusion.15), channel_id=1, source_target_pairs={{0,64},{4,68},{8,72},{12,76},{16,80},{20,84},{24,88},{28,92},{32,9... | collective-permute-start | bytes 196616 | tf_op jit(solution)/shard_map/ppermute | solution.py:8
  135.2 6.8 %collective-permute-start.12 = (bf16[1,16,2048]{2,1,0:T(8,128)(2,1)S(1)}, bf16[1,16,2048]{2,1,0:T(8,128)(2,1)S(1)}, u32[]{:S(2)}, u32[]{:S(2)}) collective-permute-start(bf16[1,16,2048]{2,1,0:T(8,128)(2,1)S(1)} %broadcast_select_fusion.23), channel_id=1, source_target_pairs={{0,128},{4,132},{8,136},{12,140},{16,144},{20,148},{24,152},{28,15... | collective-permute-start | bytes 196616 | tf_op jit(solution)/shard_map/ppermute | solution.py:8
  139.3 6.5 %collective-permute-start.24 = (bf16[1,16,2048]{2,1,0:T(8,128)(2,1)S(1)}, bf16[1,16,2048]{2,1,0:T(8,128)(2,1)S(1)}, u32[]{:S(2)}, u32[]{:S(2)}) collective-permute-start(bf16[1,16,2048]{2,1,0:T(8,128)(2,1)S(1)} %broadcast_select_fusion.16), channel_id=1, source_target_pairs={{0,128},{4,132},{8,136},{12,140},{16,144},{20,148},{24,152},{28,15... | collective-permute-start | bytes 196616 | tf_op jit(solution)/shard_map/ppermute | solution.py:8
  142.1 7.0 %collective-permute-start.13 = (bf16[1,16,2048]{2,1,0:T(8,128)(2,1)S(1)}, bf16[1,16,2048]{2,1,0:T(8,128)(2,1)S(1)}, u32[]{:S(2)}, u32[]{:S(2)}) collective-permute-start(bf16[1,16,2048]{2,1,0:T(8,128)(2,1)S(1)} %broadcast_select_fusion.24), channel_id=1, source_target_pairs={{0,256},{4,260},{8,264},{12,268},{16,272},{20,276},{24,280},{28,28... | collective-permute-start | bytes 196616 | tf_op jit(solution)/shard_map/ppermute | solution.py:8
  145.8 13.1 %collective-permute-start.25 = (bf16[1,16,2048]{2,1,0:T(8,128)(2,1)S(1)}, bf16[1,16,2048]{2,1,0:T(8,128)(2,1)S(1)}, u32[]{:S(2)}, u32[]{:S(2)}) collective-permute-start(bf16[1,16,2048]{2,1,0:T(8,128)(2,1)S(1)} %broadcast_select_fusion.17), channel_id=1, source_target_pairs={{0,256},{4,260},{8,264},{12,268},{16,272},{20,276},{24,280},{28,28... | collective-permute-start | bytes 196616 | tf_op jit(solution)/shard_map/ppermute | solution.py:8
  221.8 60.5 %collective-permute-start.33 = (f32[1,8,2,2048]{3,2,1,0:T(2,128)S(1)}, f32[1,8,2,2048]{3,2,1,0:T(2,128)S(1)}, u32[]{:S(2)}, u32[]{:S(2)}) collective-permute-start(f32[1,8,2,2048]{3,2,1,0:T(2,128)S(1)} %copy.11), channel_id=1, source_target_pairs={{0,4},{4,0},{8,12},{12,8},{16,20},{20,16},{24,28},{28,24},{32,36},... | collective-permute-start | bytes 393224 | tf_op jit(solution)/shard_map/ppermute | solution.py:8
  279.6 6.5 %collective-permute-start.26 = (f32[1,8,2,2048]{3,2,1,0:T(2,128)S(1)}, f32[1,8,2,2048]{3,2,1,0:T(2,128)S(1)}, u32[]{:S(2)}, u32[]{:S(2)}) collective-permute-start(f32[1,8,2,2048]{3,2,1,0:T(2,128)S(1)} %copy.9), channel_id=1, source_target_pairs={{0,4},{4,0},{8,12},{12,8},{16,20},{20,16},{24,28},{28,24},{32,36},... | collective-permute-start | bytes 393224 | tf_op jit(solution)/shard_map/ppermute | solution.py:8
  282.4 13.3 %collective-permute-start.34 = (f32[1,8,2,2048]{3,2,1,0:T(2,128)S(1)}, f32[1,8,2,2048]{3,2,1,0:T(2,128)S(1)}, u32[]{:S(2)}, u32[]{:S(2)}) collective-permute-start(f32[1,8,2,2048]{3,2,1,0:T(2,128)S(1)} %broadcast_select_fusion), channel_id=1, source_target_pairs={{0,8},{4,12},{8,0},{12,4},{16,24},{20,28},{24,16},{28,20},{32,40},... | collective-permute-start | bytes 393224 | tf_op jit(solution)/shard_map/ppermute | solution.py:8
  286.3 12.3 %collective-permute-start.27 = (f32[1,8,2,2048]{3,2,1,0:T(2,128)S(1)}, f32[1,8,2,2048]{3,2,1,0:T(2,128)S(1)}, u32[]{:S(2)}, u32[]{:S(2)}) collective-permute-start(f32[1,8,2,2048]{3,2,1,0:T(2,128)S(1)} %broadcast_select_fusion.6), channel_id=1, source_target_pairs={{0,8},{4,12},{8,0},{12,4},{16,24},{20,28},{24,16},{28,20},{32,40},... | collective-permute-start | bytes 393224 | tf_op jit(solution)/shard_map/ppermute | solution.py:8
  295.8 27.9 %collective-permute-start.35 = (f32[1,8,2,2048]{3,2,1,0:T(2,128)S(1)}, f32[1,8,2,2048]{3,2,1,0:T(2,128)S(1)}, u32[]{:S(2)}, u32[]{:S(2)}) collective-permute-start(f32[1,8,2,2048]{3,2,1,0:T(2,128)S(1)} %bitcast.156), channel_id=1, source_target_pairs={{0,16},{4,20},{8,24},{12,28},{16,0},{20,4},{24,8},{28,12},{32,48},... | collective-permute-start | bytes 393224 | tf_op jit(solution)/shard_map/ppermute | solution.py:8
  298.6 34.0 %collective-permute-start.28 = (f32[1,8,2,2048]{3,2,1,0:T(2,128)S(1)}, f32[1,8,2,2048]{3,2,1,0:T(2,128)S(1)}, u32[]{:S(2)}, u32[]{:S(2)}) collective-permute-start(f32[1,8,2,2048]{3,2,1,0:T(2,128)S(1)} %bitcast.157), channel_id=1, source_target_pairs={{0,16},{4,20},{8,24},{12,28},{16,0},{20,4},{24,8},{28,12},{32,48},... | collective-permute-start | bytes 393224 | tf_op jit(solution)/shard_map/ppermute | solution.py:8
  323.7 28.4 %collective-permute-start.36 = (f32[1,8,2,2048]{3,2,1,0:T(2,128)S(1)}, f32[1,8,2,2048]{3,2,1,0:T(2,128)S(1)}, u32[]{:S(2)}, u32[]{:S(2)}) collective-permute-start(f32[1,8,2,2048]{3,2,1,0:T(2,128)S(1)} %bitcast.158), channel_id=1, source_target_pairs={{0,32},{4,36},{8,40},{12,44},{16,48},{20,52},{24,56},{28,60},{32,0... | collective-permute-start | bytes 393224 | tf_op jit(solution)/shard_map/ppermute | solution.py:8
  332.6 22.3 %collective-permute-start.29 = (f32[1,8,2,2048]{3,2,1,0:T(2,128)S(1)}, f32[1,8,2,2048]{3,2,1,0:T(2,128)S(1)}, u32[]{:S(2)}, u32[]{:S(2)}) collective-permute-start(f32[1,8,2,2048]{3,2,1,0:T(2,128)S(1)} %bitcast.159), channel_id=1, source_target_pairs={{0,32},{4,36},{8,40},{12,44},{16,48},{20,52},{24,56},{28,60},{32,0... | collective-permute-start | bytes 393224 | tf_op jit(solution)/shard_map/ppermute | solution.py:8
  352.1 6.3 %collective-permute-start.37 = (f32[1,8,2,2048]{3,2,1,0:T(2,128)S(1)}, f32[1,8,2,2048]{3,2,1,0:T(2,128)S(1)}, u32[]{:S(2)}, u32[]{:S(2)}) collective-permute-start(f32[1,8,2,2048]{3,2,1,0:T(2,128)S(1)} %bitcast.160), channel_id=1, source_target_pairs={{0,64},{4,68},{8,72},{12,76},{16,80},{20,84},{24,88},{28,92},{32,9... | collective-permute-start | bytes 393224 | tf_op jit(solution)/shard_map/ppermute | solution.py:8
  354.9 6.5 %collective-permute-start.30 = (f32[1,8,2,2048]{3,2,1,0:T(2,128)S(1)}, f32[1,8,2,2048]{3,2,1,0:T(2,128)S(1)}, u32[]{:S(2)}, u32[]{:S(2)}) collective-permute-start(f32[1,8,2,2048]{3,2,1,0:T(2,128)S(1)} %bitcast.161), channel_id=1, source_target_pairs={{0,64},{4,68},{8,72},{12,76},{16,80},{20,84},{24,88},{28,92},{32,9... | collective-permute-start | bytes 393224 | tf_op jit(solution)/shard_map/ppermute | solution.py:8
  358.5 7.2 %collective-permute-start.38 = (f32[1,8,2,2048]{3,2,1,0:T(2,128)S(1)}, f32[1,8,2,2048]{3,2,1,0:T(2,128)S(1)}, u32[]{:S(2)}, u32[]{:S(2)}) collective-permute-start(f32[1,8,2,2048]{3,2,1,0:T(2,128)S(1)} %bitcast.162), channel_id=1, source_target_pairs={{0,128},{4,132},{8,136},{12,140},{16,144},{20,148},{24,152},{28,15... | collective-permute-start | bytes 393224 | tf_op jit(solution)/shard_map/ppermute | solution.py:8
  361.4 7.6 %collective-permute-start.31 = (f32[1,8,2,2048]{3,2,1,0:T(2,128)S(1)}, f32[1,8,2,2048]{3,2,1,0:T(2,128)S(1)}, u32[]{:S(2)}, u32[]{:S(2)}) collective-permute-start(f32[1,8,2,2048]{3,2,1,0:T(2,128)S(1)} %bitcast.163), channel_id=1, source_target_pairs={{0,128},{4,132},{8,136},{12,140},{16,144},{20,148},{24,152},{28,15... | collective-permute-start | bytes 393224 | tf_op jit(solution)/shard_map/ppermute | solution.py:8
  365.7 6.1 %collective-permute-start.39 = (f32[1,8,2,2048]{3,2,1,0:T(2,128)S(1)}, f32[1,8,2,2048]{3,2,1,0:T(2,128)S(1)}, u32[]{:S(2)}, u32[]{:S(2)}) collective-permute-start(f32[1,8,2,2048]{3,2,1,0:T(2,128)S(1)} %bitcast.168), channel_id=1, source_target_pairs={{0,256},{4,260},{8,264},{12,268},{16,272},{20,276},{24,280},{28,28... | collective-permute-start | bytes 393224 | tf_op jit(solution)/shard_map/ppermute | solution.py:8
  369.1 7.3 %collective-permute-start.32 = (f32[1,8,2,2048]{3,2,1,0:T(2,128)S(1)}, f32[1,8,2,2048]{3,2,1,0:T(2,128)S(1)}, u32[]{:S(2)}, u32[]{:S(2)}) collective-permute-start(f32[1,8,2,2048]{3,2,1,0:T(2,128)S(1)} %bitcast.164), channel_id=1, source_target_pairs={{0,256},{4,260},{8,264},{12,268},{16,272},{20,276},{24,280},{28,28... | collective-permute-start | bytes 393224 | tf_op jit(solution)/shard_map/ppermute | solution.py:8
Sparse Core Ops, SparseCore 0:
  377.8 39.7 reduce-scatter.1
where the time goes:
time: 427 us; the launch traced here: 426 us
  starting transfers between devices  156 us (37%)
  matrix products  105 us (25%)
  waiting for transfers between devices  88.2 us (21%)
  blocking collectives  38.1 us (9%)
  between operations  25.2 us (6%)
  local copies, waits for them, and re-layouts  9.14 us (2%)
    ppermute x40, starting transfers between devices, from_partner(): lax.ppermute(shard, axis, [(i, i ^ 1 << stride) for i in range(lax.axis_s...  156 us
    dot_general x64, matrix products, col_step(): lax.dot_general(row_scaled, col_scaled, (((0,), (0,)), ((), ())), precisi...  77 us
    ppermute x40, waiting for transfers between devices, from_partner(): lax.ppermute(shard, axis, [(i, i ^ 1 << stride) for i in range(lax.axis_s...  48.3 us
    reduce_scatter x1, waiting for transfers between devices, shards(): lax.psum_scatter(spread, 'pair', scatter_dimension=0, tiled=True)[0]  39.9 us
    all_gather x2, blocking collectives, shards(): lax.all_gather(far_vals[round_index], 'pair', axis=1, tiled=True)  20.9 us
    all_gather x2, blocking collectives, shards(): lax.all_gather(far_pts[round_index], 'pair', axis=1, tiled=True)  17.2 us
    dot_general x64, matrix products, col_step(): tile_piece = jnp.dot(row_vals, kernel, preferred_element_type=jnp.float32)  15.7 us
    dot_general x64, matrix products, col_step(): lax.dot_general(col_vals, kernel, (((1,), (1,)), ((), ())), preferred_ele...  11 us
  transfers between devices with their start and end apart: 41, of which 14 were waited for; matrix products, arithmetic and copies ran while one was open for 14% of the time, Pallas kernels for 0%

commit v1 on v0

v1 whole, which is shorter than its diff:
```python
import functools
import math

import jax
import jax.numpy as jnp
from jax import lax
from jax.experimental import pallas as pl
from jax.experimental.pallas import tpu as pltpu
from jax.sharding import PartitionSpec as P

LOG2E = math.log2(math.e)
DEPTH = 64
ROW_TILE = 1024


def split3(x):
    high = x.astype(jnp.bfloat16)
    rest = x - high.astype(jnp.float32)
    mid = rest.astype(jnp.bfloat16)
    low = (rest - mid.astype(jnp.float32)).astype(jnp.bfloat16)
    return high, mid, low


def half_norm(pts, inv_sq):
    return jnp.sum(pts * pts * inv_sq, axis=0, keepdims=True) * (-0.5 * LOG2E)


def norm_rows(own_first, norm):
    pieces = [p.astype(jnp.float32) for p in split3(norm)]
    row = lax.broadcasted_iota(jnp.int32, (16, norm.shape[1]), 0)
    start = 0 if own_first else 3
    other = 3 - start
    out = jnp.where((row >= other) & (row < other + 3), 1.0, 0.0)
    for i, piece in enumerate(pieces):
        out = jnp.where(row == start + i, piece, out)
    return out.astype(jnp.bfloat16)


def product_kernel(own_ref, ls_ref, far_ref, out_ref, own_side, far_side, far_rows):
    rounds, quarters, _, count = far_ref.shape
    scale = ls_ref[...]
    inv_sq = 1.0 / (scale * scale)
    own = own_ref[...].astype(jnp.float32)
    for i, piece in enumerate(split3(own * (inv_sq * LOG2E))):
        own_side[16 * i : 16 * i + 16, :] = piece
    own_side[48:64, :] = norm_rows(True, half_norm(own, inv_sq))
    out_ref[...] = jnp.zeros_like(out_ref)

    def step(index, carry):
        data = far_ref.at[index // quarters, index % quarters]
        raw = data[0:16, :]
        for i in range(3):
            far_side[16 * i : 16 * i + 16, :] = raw
        far_side[48:64, :] = norm_rows(False, half_norm(raw.astype(jnp.float32), inv_sq))
        far_rows[...] = far_side[...].T

        def tile(part, total):
            first = pl.multiple_of(part * ROW_TILE, ROW_TILE)
            power = jnp.dot(
                far_rows[pl.ds(first, ROW_TILE), :], own_side[...], preferred_element_type=jnp.float32
            )
            block = jnp.exp2(power).astype(jnp.bfloat16)
            vals = data[16:24, pl.ds(first, ROW_TILE)]
            return total + jnp.dot(vals, block, preferred_element_type=jnp.float32)

        out_ref[...] = lax.fori_loop(0, count // ROW_TILE, tile, out_ref[...])
        return carry

    lax.fori_loop(0, rounds * quarters, step, 0)


def block_product(own, scales, far):
    count = own.shape[1]
    return pl.pallas_call(
        product_kernel,
        out_shape=jax.ShapeDtypeStruct((8, count), jnp.float32),
        scratch_shapes=[
            pltpu.VMEM((DEPTH, count), jnp.bfloat16),
            pltpu.VMEM((DEPTH, count), jnp.bfloat16),
            pltpu.VMEM((count, DEPTH), jnp.bfloat16),
        ],
        compiler_params=pltpu.CompilerParams(vmem_limit_bytes=48 << 20),
    )(own, scales, far)


def move(mask, shard):
    return lax.ppermute(shard, "blk", [(i, i ^ mask) for i in range(lax.axis_size("blk"))])


def shards(points, values, length_scales, partners):
    blocks = lax.axis_size("blk")
    masks = jnp.bitwise_xor(partners[:, 0], lax.axis_index("blk"))
    mine = jnp.concatenate([points, values], 0)
    branches = [functools.partial(move, mask) for mask in range(blocks)]
    far = jnp.stack([lax.switch(masks[r], branches, mine) for r in range(partners.shape[0])])
    far = lax.all_gather(far, "pair", axis=1)
    return block_product(points, length_scales[:, None], far)


def solution(mesh):
    placed = (P(None, ("blk", "pair")), P(None, ("blk", "pair")), P(), P(None, "blk"))
    return jax.shard_map(
        shards, mesh=mesh, in_specs=placed, out_specs=P(None, ("blk", "pair")), check_vma=False
    )
```

time: 427 us -> 128 us (0.30)
  starting transfers between devices: 156 us -> 34.7 us
  matrix products: 105 us -> 0 us
  waiting for transfers between devices: 88.2 us -> 41.5 us
  Pallas kernels: 0 us -> 30.4 us
  between operations: 25.2 us -> 1.39 us
  blocking collectives: 38.1 us -> 15.1 us
  local copies, waits for them, and re-layouts: 9.14 us -> 2.92 us
    ppermute x40 -> x2, starting transfers between devices: 156 us -> 34.7 us  [move(): lax.ppermute(shard, 'blk', [(i, i ^ mask) for i in range(lax.axis_size('b...]
    dot_general x194 -> x0, matrix products: 105 us -> none  [the longest x64 77 us: col_step(): lax.dot_general(row_scaled, col_scaled, (((0,), (0,)), ((), ())), precisi...]
    reduce_scatter x1 -> x0, waiting for transfers between devices: 39.9 us -> none  [shards(): lax.psum_scatter(spread, 'pair', scatter_dimension=0, tiled=True)[0]]
    pallas_call x0 -> x1, Pallas kernels: none -> 30.4 us  [block_product(): pl.pallas_call(product_kernel, out_shape=jax.ShapeDtypeStruct((8, count),...]
    all_gather x4 -> x1, blocking collectives: 38.1 us -> 15.1 us  [shards(): far = lax.all_gather(far, 'pair', axis=1)]
    ppermute x40 -> x2, waiting for transfers between devices: 48.3 us -> 41.5 us  [move(): lax.ppermute(shard, 'blk', [(i, i ^ mask) for i in range(lax.axis_size('b...]
    dynamic_slice x92 -> x0, local copies, waits for them, and re-layouts: 5.52 us -> none  [the longest x64 4.75 us: col_step(): lax.dynamic_slice_in_dim(far_sq, col_index * block_step, block_step, 0)]
  transfers between devices with their start and end apart: 41 -> 2, of which waited for: 14 -> 2; matrix products, arithmetic and copies ran while one was open for 14% -> 0% of each run, Pallas kernels for 0% -> 0%
where the time goes in v1:
time: 128 us; the launch traced here: 127 us
  waiting for transfers between devices  41.5 us (32%)
  starting transfers between devices  34.7 us (27%)
  Pallas kernels  30.4 us (24%)
  blocking collectives  15.1 us (12%)
  local copies, waits for them, and re-layouts  2.92 us (2%)
  between operations  1.39 us (1%)
    ppermute x2, waiting for transfers between devices, move(): lax.ppermute(shard, 'blk', [(i, i ^ mask) for i in range(lax.axis_size('b...  41.5 us
    ppermute x2, starting transfers between devices, move(): lax.ppermute(shard, 'blk', [(i, i ^ mask) for i in range(lax.axis_size('b...  34.7 us
    pallas_call x1, Pallas kernels, block_product(): pl.pallas_call(product_kernel, out_shape=jax.ShapeDtypeStruct((8, count),...  30.4 us
    all_gather x1, blocking collectives, shards(): far = lax.all_gather(far, 'pair', axis=1)  15.1 us
  transfers between devices with their start and end apart: 2, of which 2 were waited for; matrix products, arithmetic and copies ran while one was open for 0% of the time, Pallas kernels for 0%

profile of v1, /device:TPU:1, one launch (start us, length us, event | category | flops | bytes accessed | tf_op | source)
XLA Modules:
  0.0 127.4 jit_solution(12022413688296451885)
XLA Ops:
  0.0 0.0 copy-start.1
  0.0 0.9 constant_dynamic-update-slice_fusion.1
  0.9 0.0 copy-done.1
  0.9 0.0 copy-start.3
  0.9 0.6 copy-done.3
  1.5 0.7 fusion
  2.8 39.1 %conditional.2 = (bf16[1,24,2048]{2,1,0:T(8,128)(2,1)}) conditional(s32[]{:T(128)} %bitcast.257, bf16[24,2048]{1,0:T(8,128)(2,1)S(1)} %constant_dynamic-update-slice_fusion, bf16[24,2048]{1,0:T(8,128)(2,1)S(1)} %constant_dynamic-update-slice_fusion, ...), branch_computations={%region_0.0_spmd, %region_1.0_spmd, %region_2.0_spmd, %region_3.0_... | conditional | bytes 393264 | solution.py:95
  2.9 21.7 %collective-permute-start.91 = (bf16[24,2048]{1,0:T(8,128)(2,1)S(1)}, bf16[24,2048]{1,0:T(8,128)(2,1)}, u32[]{:S(2)}, u32[]{:S(2)}) collective-permute-start(bf16[24,2048]{1,0:T(8,128)(2,1)S(1)} %param.91), channel_id=1, source_target_pairs={{0,364},{4,360},{8,356},{12,352},{16,380},{20,376},{24,372},{28,36... | collective-permute-start | bytes 294920 | tf_op jit(solution)/shard_map/cond/branch_91_fun/ppermute | solution.py:87
  24.6 17.4 %collective-permute-done.91 = bf16[24,2048]{1,0:T(8,128)(2,1)} collective-permute-done((bf16[24,2048]{1,0:T(8,128)(2,1)S(1)}, bf16[24,2048]{1,0:T(8,128)(2,1)}, u32[]{:S(2)}, u32[]{:S(2)}) %collective-permute-start.91) | collective-permute-done | bytes 98336 | tf_op jit(solution)/shard_map/cond/branch_91_fun/ppermute | solution.py:87
  42.6 37.4 %conditional.3 = (bf16[1,24,2048]{2,1,0:T(8,128)(2,1)}) conditional(s32[]{:T(128)} %bitcast.258, bf16[24,2048]{1,0:T(8,128)(2,1)S(1)} %constant_dynamic-update-slice_fusion, bf16[24,2048]{1,0:T(8,128)(2,1)S(1)} %constant_dynamic-update-slice_fusion, ...), branch_computations={%region_128.0_spmd, %region_129.0_spmd, %region_130.0_spmd, %regio... | conditional | bytes 393264 | solution.py:95
  42.9 13.0 %collective-permute-start.233 = (bf16[24,2048]{1,0:T(8,128)(2,1)S(1)}, bf16[24,2048]{1,0:T(8,128)(2,1)}, u32[]{:S(2)}, u32[]{:S(2)}) collective-permute-start(bf16[24,2048]{1,0:T(8,128)(2,1)S(1)} %param.233), channel_id=1, source_target_pairs={{0,420},{4,416},{8,428},{12,424},{16,436},{20,432},{24,444},{28,44... | collective-permute-start | bytes 294920 | tf_op jit(solution)/shard_map/cond/branch_105_fun/ppermute | solution.py:87
  55.9 24.2 %collective-permute-done.233 = bf16[24,2048]{1,0:T(8,128)(2,1)} collective-permute-done((bf16[24,2048]{1,0:T(8,128)(2,1)S(1)}, bf16[24,2048]{1,0:T(8,128)(2,1)}, u32[]{:S(2)}, u32[]{:S(2)}) %collective-permute-start.233) | collective-permute-done | bytes 98336 | tf_op jit(solution)/shard_map/cond/branch_105_fun/ppermute | solution.py:87
  80.1 1.0 pad_maximum_fusion
  81.1 0.0 copy-start
  81.1 15.1 %all-gather = bf16[2,96,2048]{2,1,0:T(8,128)(2,1)S(1)} all-gather(bf16[2,24,2048]{2,1,0:T(8,128)(2,1)S(1)} %pad_maximum_fusion), channel_id=2, replica_groups=mesh['blk'=128,'pair'=4] {'pair'}, dimensions={1}, use_global_device_ids=true | all-gather | bytes 983040 | tf_op jit(solution)/shard_map/all_gather | solution.py:96
  96.2 0.0 copy-start.2
  96.2 0.7 copy-done.2
  96.9 0.1 copy.5.ls_ref
  96.9 0.0 copy-done
  96.9 30.4 %shard_map.46 = f32[8,2048]{1,0:T(8,128)} custom-call(bf16[16,2048]{1,0:T(8,128)(2,1)S(1)} %copy-done, f32[16,1]{1,0:T(8,128)S(1)} %copy.5.ls_ref, bf16[2,4,24,2048]{3,2,1,0:T(8,128)(2,1)S(1)} %bitcast.260), custom_call_target="tpu_custom_call" | custom-call | tf_op jit(solution)/shard_map/pallas_call | solution.py:74
  (2 shorter events, 0.0 us)
Async XLA Ops:
  0.0 0.9 copy-start.1
  0.9 0.7 copy-start.3
  2.9 39.1 %collective-permute-start.91 = (bf16[24,2048]{1,0:T(8,128)(2,1)S(1)}, bf16[24,2048]{1,0:T(8,128)(2,1)}, u32[]{:S(2)}, u32[]{:S(2)}) collective-permute-start(bf16[24,2048]{1,0:T(8,128)(2,1)S(1)} %param.91), channel_id=1, source_target_pairs={{0,364},{4,360},{8,356},{12,352},{16,380},{20,376},{24,372},{28,36... | collective-permute-start | bytes 294920 | tf_op jit(solution)/shard_map/cond/branch_91_fun/ppermute | solution.py:87
  42.9 37.2 %collective-permute-start.233 = (bf16[24,2048]{1,0:T(8,128)(2,1)S(1)}, bf16[24,2048]{1,0:T(8,128)(2,1)}, u32[]{:S(2)}, u32[]{:S(2)}) collective-permute-start(bf16[24,2048]{1,0:T(8,128)(2,1)S(1)} %param.233), channel_id=1, source_target_pairs={{0,420},{4,416},{8,428},{12,424},{16,436},{20,432},{24,444},{28,44... | collective-permute-start | bytes 294920 | tf_op jit(solution)/shard_map/cond/branch_105_fun/ppermute | solution.py:87
  81.1 15.9 %copy-start = (bf16[16,2048]{1,0:T(8,128)(2,1)S(1)}, bf16[16,2048]{1,0:T(8,128)(2,1)}, u32[]{:S(2)}) copy-start(bf16[16,2048]{1,0:T(8,128)(2,1)} %own_ref.1) | copy-start | bytes 196612
  96.2 0.7 copy-start.2

commit v2 on v1

--- a/solution.py
+++ b/solution.py
@@ -84,16 +84,27 @@
 
 
 def move(mask, shard):
+    if mask == 0:
+        return shard
     return lax.ppermute(shard, "blk", [(i, i ^ mask) for i in range(lax.axis_size("blk"))])
 
 
+def hop(shard, mask, first_bit, bits):
+    index = jnp.bitwise_and(jnp.right_shift(mask, first_bit), (1 << bits) - 1)
+    return lax.switch(index, [functools.partial(move, k << first_bit) for k in range(1 << bits)], shard)
+
+
 def shards(points, values, length_scales, partners):
-    blocks = lax.axis_size("blk")
-    masks = jnp.bitwise_xor(partners[:, 0], lax.axis_index("blk"))
+    bits = lax.axis_size("blk").bit_length() - 1
+    near = 3
+    round_index = jnp.bitwise_and(lax.axis_index("pair"), 1)
+    mask = jnp.bitwise_xor(jnp.where(round_index == 0, partners[0, 0], partners[1, 0]), lax.axis_index("blk"))
     mine = jnp.concatenate([points, values], 0)
-    branches = [functools.partial(move, mask) for mask in range(blocks)]
-    far = jnp.stack([lax.switch(masks[r], branches, mine) for r in range(partners.shape[0])])
-    far = lax.all_gather(far, "pair", axis=1)
+    sibling = lax.ppermute(mine, "pair", [(i, i ^ 1) for i in range(lax.axis_size("pair"))])
+    far = jnp.stack([mine, sibling])
+    far = hop(far, mask, bits - near, near)
+    far = hop(far, mask, 0, bits - near)
+    far = lax.all_gather(far, "pair", axis=0)
     return block_product(points, length_scales[:, None], far)
 
 

time: 128 us -> 77.4 us (0.60)
  waiting for transfers between devices: 41.5 us -> 8.92 us
  starting transfers between devices: 34.7 us -> 15.4 us
  blocking collectives: 15.1 us -> 18 us
    ppermute x2 -> x1, waiting for transfers between devices: 41.5 us -> 8.91 us  [move(): lax.ppermute(shard, 'blk', [(i, i ^ mask) for i in range(lax.axis_size('b...]
    ppermute x2 -> x1, starting transfers between devices: 34.7 us -> 6.64 us  [move(): lax.ppermute(shard, 'blk', [(i, i ^ mask) for i in range(lax.axis_size('b...]
    ppermute x0 -> x1, starting transfers between devices: none -> 8.79 us  [shards(): lax.ppermute(mine, 'pair', [(i, i ^ 1) for i in range(lax.axis_size('pair...]
    all_gather x1, blocking collectives: 15.1 us -> 18 us  [shards(): far = lax.all_gather(far, 'pair', axis=0)]
  transfers between devices with their start and end apart: 2 -> 2, of which waited for: 2 -> 1; matrix products, arithmetic and copies ran while one was open for 0% -> 1% of each run, Pallas kernels for 0% -> 0%
where the time goes in v2:
time: 77.4 us; the launch traced here: 77.1 us
  Pallas kernels  30.4 us (39%)
  blocking collectives  18 us (23%)
  starting transfers between devices  15.4 us (20%)
  waiting for transfers between devices  8.92 us (12%)
  local copies, waits for them, and re-layouts  2.84 us (4%)
  between operations  1.36 us (2%)
    pallas_call x1, Pallas kernels, block_product(): pl.pallas_call(product_kernel, out_shape=jax.ShapeDtypeStruct((8, count),...  30.4 us
    all_gather x1, blocking collectives, shards(): far = lax.all_gather(far, 'pair', axis=0)  18 us
    ppermute x1, waiting for transfers between devices, move(): lax.ppermute(shard, 'blk', [(i, i ^ mask) for i in range(lax.axis_size('b...  8.91 us
    ppermute x1, starting transfers between devices, shards(): lax.ppermute(mine, 'pair', [(i, i ^ 1) for i in range(lax.axis_size('pair...  8.79 us
    ppermute x1, starting transfers between devices, move(): lax.ppermute(shard, 'blk', [(i, i ^ mask) for i in range(lax.axis_size('b...  6.64 us
    unnamed x9, local copies, waits for them, and re-layouts  2.16 us
  transfers between devices with their start and end apart: 2, of which 1 were waited for; matrix products, arithmetic and copies ran while one was open for 1% of the time, Pallas kernels for 0%

profile of v2, /device:TPU:1, one launch (start us, length us, event | category | flops | bytes accessed | tf_op | source)
XLA Modules:
  0.0 77.1 jit_solution(10143474756493458082)
XLA Ops:
  0.0 0.0 copy-start.1
  0.0 0.9 %constant_dynamic-update-slice_fusion.1 = bf16[24,2048]{1,0:T(8,128)(2,1)S(1)} fusion(bf16[16,2048]{1,0:T(8,128)(2,1)} %own_ref.1), kind=kLoop, calls=%fused_computation.2 | loop fusion | bytes 131072
  0.9 0.0 copy-done.1
  0.9 8.8 %collective-permute-start.22 = (bf16[24,2048]{1,0:T(8,128)(2,1)S(1)}, bf16[24,2048]{1,0:T(8,128)(2,1)S(1)}, u32[]{:S(2)}, u32[]{:S(2)}) collective-permute-start(bf16[24,2048]{1,0:T(8,128)(2,1)S(1)} %constant_dynamic-update-slice_fusion), channel_id=1, source_target_pairs={{0,1},{1,0},{2,3},{3,2},{4,5},{5,4},{6,7},{7,6},{8,9},{9,8},{10,11... | collective-permute-start | bytes 294920 | tf_op jit(solution)/shard_map/ppermute | solution.py:103
  9.7 0.0 copy-start.2
  9.7 0.6 copy-done.2
  10.3 0.6 fusion
  12.2 0.0 copy-start.3
  12.2 0.6 copy-done.3
  12.9 0.1 copy.6.ls_ref
  12.9 0.0 collective-permute-done.22
  13.0 15.6 %conditional.3 = (bf16[2,24,2048]{2,1,0:T(8,128)(2,1)S(1)}) conditional(s32[]{:T(128)} %clamp.6, bf16[2,24,2048]{2,1,0:T(8,128)(2,1)S(1)} %get-tuple-element.57, bf16[2,24,2048]{2,1,0:T(8,128)(2,1)S(1)} %get-tuple-element.57, bf16[2,24,2048]{2,1,0:T(8,128)(2,1)S(1)} %get-tuple-element.57, ...), branch_computations={%region_8.9_spmd, %region_9.10_spmd, %region_10.11_spmd, %region_1... | conditional | bytes 1179696 | solution.py:94
  13.1 6.6 %collective-permute-start.19 = (bf16[2,24,2048]{2,1,0:T(8,128)(2,1)S(1)}, bf16[2,24,2048]{2,1,0:T(8,128)(2,1)S(1)}, u32[]{:S(2)}, u32[]{:S(2)}) collective-permute-start(bf16[2,24,2048]{2,1,0:T(8,128)(2,1)S(1)} %param.21), channel_id=1, source_target_pairs={{0,52},{4,48},{8,60},{12,56},{16,36},{20,32},{24,44},{28,40},{32,2... | collective-permute-start | bytes 589832 | tf_op jit(solution)/shard_map/cond/branch_13_fun/ppermute | solution.py:89
  19.7 8.9 %collective-permute-done.19 = bf16[2,24,2048]{2,1,0:T(8,128)(2,1)S(1)} collective-permute-done((bf16[2,24,2048]{2,1,0:T(8,128)(2,1)S(1)}, bf16[2,24,2048]{2,1,0:T(8,128)(2,1)S(1)}, u32[]{:S(2)}, u32[]{:S(2)}) %collective-permute-start.19) | collective-permute-done | bytes 196640 | tf_op jit(solution)/shard_map/cond/branch_13_fun/ppermute | solution.py:89
  28.6 0.0 copy-start
  28.7 18.0 %all-gather = bf16[8,24,2048]{2,1,0:T(8,128)(2,1)S(1)} all-gather(bf16[2,24,2048]{2,1,0:T(8,128)(2,1)S(1)} %get-tuple-element.58), channel_id=2, replica_groups=mesh['blk'=128,'pair'=4] {'pair'}, dimensions={0}, use_global_device_ids=true | all-gather | bytes 983040 | tf_op jit(solution)/shard_map/all_gather | solution.py:107
  46.7 0.0 copy-done
  46.7 30.4 %shard_map.46 = f32[8,2048]{1,0:T(8,128)} custom-call(bf16[16,2048]{1,0:T(8,128)(2,1)S(1)} %copy-done, f32[16,1]{1,0:T(8,128)S(1)} %copy.6.ls_ref, bf16[4,2,24,2048]{3,2,1,0:T(8,128)(2,1)S(1)} %bitcast.6), custom_call_target="tpu_custom_call" | custom-call | tf_op jit(solution)/shard_map/pallas_call | solution.py:74
  (4 shorter events, 0.1 us)
Async XLA Ops:
  0.0 0.9 %copy-start.1 = (bf16[8,2048]{1,0:T(8,128)(2,1)S(1)}, bf16[8,2048]{1,0:T(8,128)(2,1)}, u32[]{:S(2)}) copy-start(bf16[8,2048]{1,0:T(8,128)(2,1)} %param.29) | copy-start | bytes 98308
  0.9 12.1 %collective-permute-start.22 = (bf16[24,2048]{1,0:T(8,128)(2,1)S(1)}, bf16[24,2048]{1,0:T(8,128)(2,1)S(1)}, u32[]{:S(2)}, u32[]{:S(2)}) collective-permute-start(bf16[24,2048]{1,0:T(8,128)(2,1)S(1)} %constant_dynamic-update-slice_fusion), channel_id=1, source_target_pairs={{0,1},{1,0},{2,3},{3,2},{4,5},{5,4},{6,7},{7,6},{8,9},{9,8},{10,11... | collective-permute-start | bytes 294920 | tf_op jit(solution)/shard_map/ppermute | solution.py:103
  9.7 0.7 copy-start.2
  12.2 0.7 copy-start.3
  13.1 15.6 %collective-permute-start.19 = (bf16[2,24,2048]{2,1,0:T(8,128)(2,1)S(1)}, bf16[2,24,2048]{2,1,0:T(8,128)(2,1)S(1)}, u32[]{:S(2)}, u32[]{:S(2)}) collective-permute-start(bf16[2,24,2048]{2,1,0:T(8,128)(2,1)S(1)} %param.21), channel_id=1, source_target_pairs={{0,52},{4,48},{8,60},{12,56},{16,36},{20,32},{24,44},{28,40},{32,2... | collective-permute-start | bytes 589832 | tf_op jit(solution)/shard_map/cond/branch_13_fun/ppermute | solution.py:89
  28.6 18.0 %copy-start = (bf16[16,2048]{1,0:T(8,128)(2,1)S(1)}, bf16[16,2048]{1,0:T(8,128)(2,1)}, u32[]{:S(2)}) copy-start(bf16[16,2048]{1,0:T(8,128)(2,1)} %own_ref.1) | copy-start | bytes 196612

commit v3 on v2

--- a/solution.py
+++ b/solution.py
@@ -10,7 +10,7 @@
 
 LOG2E = math.log2(math.e)
 DEPTH = 64
-ROW_TILE = 1024
+ROW_TILE = 512
 
 
 def split3(x):
@@ -36,51 +36,64 @@
     return out.astype(jnp.bfloat16)
 
 
-def product_kernel(own_ref, ls_ref, far_ref, out_ref, own_side, far_side, far_rows):
-    rounds, quarters, _, count = far_ref.shape
-    scale = ls_ref[...]
+def own_rows(points, inv_sq):
+    pts = points.astype(jnp.float32)
+    pieces = list(split3(pts * (inv_sq * LOG2E)))
+    return jnp.concatenate(pieces + [norm_rows(True, half_norm(pts, inv_sq))], 0)
+
+
+def far_prepare(raw, inv_sq, side, rows):
+    for i in range(3):
+        side[16 * i : 16 * i + 16, :] = raw
+    side[48:64, :] = norm_rows(False, half_norm(raw.astype(jnp.float32), inv_sq))
+    rows[...] = side[...].T
+
+
+def add_unit(total, rows, own_side, vals):
+    for first in range(0, rows.shape[0], ROW_TILE):
+        part = slice(first, first + ROW_TILE)
+        power = jnp.dot(rows[part, :], own_side[...], preferred_element_type=jnp.float32)
+        block = jnp.exp2(power).astype(jnp.bfloat16)
+        total = total + jnp.dot(vals[:, part], block, preferred_element_type=jnp.float32)
+    return total
+
+
+def product_kernel(scales, own_ref, far_ref, out_ref, own_side, side_a, rows_a, side_b, rows_b):
+    units = far_ref.shape[0]
+    feature = lax.broadcasted_iota(jnp.int32, (16, 1), 0)
+    scale = jnp.ones((16, 1), jnp.float32)
+    for i in range(16):
+        scale = jnp.where(feature == i, scales[i], scale)
     inv_sq = 1.0 / (scale * scale)
-    own = own_ref[...].astype(jnp.float32)
-    for i, piece in enumerate(split3(own * (inv_sq * LOG2E))):
-        own_side[16 * i : 16 * i + 16, :] = piece
-    own_side[48:64, :] = norm_rows(True, half_norm(own, inv_sq))
+    own_side[...] = own_rows(own_ref[...], inv_sq)
     out_ref[...] = jnp.zeros_like(out_ref)
+    far_prepare(far_ref[0, 0:16, :], inv_sq, side_a, rows_a)
 
-    def step(index, carry):
-        data = far_ref.at[index // quarters, index % quarters]
-        raw = data[0:16, :]
-        for i in range(3):
-            far_side[16 * i : 16 * i + 16, :] = raw
-        far_side[48:64, :] = norm_rows(False, half_norm(raw.astype(jnp.float32), inv_sq))
-        far_rows[...] = far_side[...].T
-
-        def tile(part, total):
-            first = pl.multiple_of(part * ROW_TILE, ROW_TILE)
-            power = jnp.dot(
-                far_rows[pl.ds(first, ROW_TILE), :], own_side[...], preferred_element_type=jnp.float32
-            )
-            block = jnp.exp2(power).astype(jnp.bfloat16)
-            vals = data[16:24, pl.ds(first, ROW_TILE)]
-            return total + jnp.dot(vals, block, preferred_element_type=jnp.float32)
-
-        out_ref[...] = lax.fori_loop(0, count // ROW_TILE, tile, out_ref[...])
+    def two_units(pair, carry):
+        first = 2 * pair
+        far_prepare(far_ref[first + 1, 0:16, :], inv_sq, side_b, rows_b)
+        total = add_unit(out_ref[...], rows_a, own_side, far_ref[first, 16:24, :])
+        later = lax.rem(first + 2, units)
+        far_prepare(far_ref[later, 0:16, :], inv_sq, side_a, rows_a)
+        out_ref[...] = add_unit(total, rows_b, own_side, far_ref[first + 1, 16:24, :])
         return carry
 
-    lax.fori_loop(0, rounds * quarters, step, 0)
+    lax.fori_loop(0, units // 2, two_units, 0)
 
 
 def block_product(own, scales, far):
     count = own.shape[1]
+    side = pltpu.VMEM((DEPTH, count), jnp.bfloat16)
+    rows = pltpu.VMEM((count, DEPTH), jnp.bfloat16)
+    in_vmem = pl.BlockSpec(memory_space=pltpu.VMEM)
     return pl.pallas_call(
         product_kernel,
         out_shape=jax.ShapeDtypeStruct((8, count), jnp.float32),
-        scratch_shapes=[
-            pltpu.VMEM((DEPTH, count), jnp.bfloat16),
-            pltpu.VMEM((DEPTH, count), jnp.bfloat16),
-            pltpu.VMEM((count, DEPTH), jnp.bfloat16),
-        ],
+        in_specs=[pl.BlockSpec(memory_space=pltpu.SMEM), in_vmem, in_vmem],
+        out_specs=in_vmem,
+        scratch_shapes=[side, side, rows, side, rows],
         compiler_params=pltpu.CompilerParams(vmem_limit_bytes=48 << 20),
-    )(own, scales, far)
+    )(scales, own, far)
 
 
 def move(mask, shard):
@@ -105,7 +118,7 @@
     far = hop(far, mask, bits - near, near)
     far = hop(far, mask, 0, bits - near)
     far = lax.all_gather(far, "pair", axis=0)
-    return block_product(points, length_scales[:, None], far)
+    return block_product(points, length_scales, far.reshape((-1,) + mine.shape))
 
 
 def solution(mesh):

time: 77.4 us -> 72.6 us (0.938)
  blocking collectives: 18 us -> 8.11 us
  waiting for transfers between devices: 8.92 us -> 17 us
  Pallas kernels: 30.4 us -> 27.8 us
    all_gather x1, blocking collectives: 18 us -> 8.11 us  [shards(): far = lax.all_gather(far, 'pair', axis=0)]
    ppermute x1 -> x2, waiting for transfers between devices: 8.91 us -> 17 us  [move(): lax.ppermute(shard, 'blk', [(i, i ^ mask) for i in range(lax.axis_size('b...]
    pallas_call x1, Pallas kernels: 30.4 us -> 27.8 us  [block_product(): pl.pallas_call(product_kernel, out_shape=jax.ShapeDtypeStruct((8, count),...]
    ppermute x1 -> x2, starting transfers between devices: 6.64 us -> 6.8 us  [move(): lax.ppermute(shard, 'blk', [(i, i ^ mask) for i in range(lax.axis_size('b...]
  transfers between devices with their start and end apart: 2 -> 3, of which waited for: 1 -> 2; matrix products, arithmetic and copies ran while one was open for 1% -> 1% of each run, Pallas kernels for 0% -> 0%
where the time goes in v3:
time: 72.6 us; the launch traced here: 72.1 us
  Pallas kernels  27.8 us (38%)
  waiting for transfers between devices  17 us (23%)
  starting transfers between devices  15.6 us (21%)
  blocking collectives  8.11 us (11%)
  local copies, waits for them, and re-layouts  2.13 us (3%)
  between operations  1.38 us (2%)
    pallas_call x1, Pallas kernels, block_product(): pl.pallas_call(product_kernel, out_shape=jax.ShapeDtypeStruct((8, count),...  27.8 us
    ppermute x2, waiting for transfers between devices, move(): lax.ppermute(shard, 'blk', [(i, i ^ mask) for i in range(lax.axis_size('b...  17 us
    ppermute x1, starting transfers between devices, shards(): lax.ppermute(mine, 'pair', [(i, i ^ 1) for i in range(lax.axis_size('pair...  8.79 us
    all_gather x1, blocking collectives, shards(): far = lax.all_gather(far, 'pair', axis=0)  8.11 us
    ppermute x2, starting transfers between devices, move(): lax.ppermute(shard, 'blk', [(i, i ^ mask) for i in range(lax.axis_size('b...  6.8 us
    unnamed x9, local copies, waits for them, and re-layouts  1.52 us
  transfers between devices with their start and end apart: 3, of which 2 were waited for; matrix products, arithmetic and copies ran while one was open for 1% of the time, Pallas kernels for 0%

profile of v3, /device:TPU:1, one launch (start us, length us, event | category | flops | bytes accessed | tf_op | source)
XLA Modules:
  0.0 72.1 jit_solution(15879829378276514634)
XLA Ops:
  0.0 0.0 copy-start.2
  0.0 0.9 %constant_dynamic-update-slice_fusion.1 = bf16[24,2048]{1,0:T(8,128)(2,1)S(1)} fusion(bf16[16,2048]{1,0:T(8,128)(2,1)} %own_ref.1), kind=kLoop, calls=%fused_computation.2 | loop fusion | bytes 131072
  0.9 0.0 copy-done.2
  0.9 8.8 %collective-permute-start.22 = (bf16[24,2048]{1,0:T(8,128)(2,1)S(1)}, bf16[24,2048]{1,0:T(8,128)(2,1)S(1)}, u32[]{:S(2)}, u32[]{:S(2)}) collective-permute-start(bf16[24,2048]{1,0:T(8,128)(2,1)S(1)} %constant_dynamic-update-slice_fusion), channel_id=1, source_target_pairs={{0,1},{1,0},{2,3},{3,2},{4,5},{5,4},{6,7},{7,6},{8,9},{9,8},{10,11... | collective-permute-start | bytes 294920 | tf_op jit(solution)/shard_map/ppermute | solution.py:116
  9.7 0.0 copy-start.3
  9.7 0.6 copy-done.3
  10.3 0.6 fusion
  12.2 0.0 collective-permute-done.22
  12.2 8.0 %conditional.2 = (bf16[2,24,2048]{2,1,0:T(8,128)(2,1)S(1)}) conditional(s32[]{:T(128)} %clamp.7, bf16[2,24,2048]{2,1,0:T(8,128)(2,1)S(1)} %pad_maximum_fusion, bf16[2,24,2048]{2,1,0:T(8,128)(2,1)S(1)} %pad_maximum_fusion, bf16[2,24,2048]{2,1,0:T(8,128)(2,1)S(1)} %pad_maximum_fusion, ...), branch_computations={%region_0.1_spmd, %region_1.2_spmd, %region_2.3_spmd, %region_3.4_... | conditional | bytes 1179696 | solution.py:107
  12.3 1.9 %collective-permute-start.1 = (bf16[2,24,2048]{2,1,0:T(8,128)(2,1)S(1)}, bf16[2,24,2048]{2,1,0:T(8,128)(2,1)S(1)}, u32[]{:S(2)}, u32[]{:S(2)}) collective-permute-start(bf16[2,24,2048]{2,1,0:T(8,128)(2,1)S(1)} %param.2), channel_id=1, source_target_pairs={{0,128},{4,132},{8,136},{12,140},{16,144},{20,148},{24,152},{28,15... | collective-permute-start | bytes 589832 | tf_op jit(solution)/shard_map/cond/branch_2_fun/ppermute | solution.py:102
  14.2 6.0 %collective-permute-done.1 = bf16[2,24,2048]{2,1,0:T(8,128)(2,1)S(1)} collective-permute-done((bf16[2,24,2048]{2,1,0:T(8,128)(2,1)S(1)}, bf16[2,24,2048]{2,1,0:T(8,128)(2,1)S(1)}, u32[]{:S(2)}, u32[]{:S(2)}) %collective-permute-start.1) | collective-permute-done | bytes 196640 | tf_op jit(solution)/shard_map/cond/branch_2_fun/ppermute | solution.py:102
  20.2 15.9 %conditional.3 = (bf16[2,24,2048]{2,1,0:T(8,128)(2,1)S(1)}) conditional(s32[]{:T(128)} %clamp.6, bf16[2,24,2048]{2,1,0:T(8,128)(2,1)S(1)} %get-tuple-element.57, bf16[2,24,2048]{2,1,0:T(8,128)(2,1)S(1)} %get-tuple-element.57, bf16[2,24,2048]{2,1,0:T(8,128)(2,1)S(1)} %get-tuple-element.57, ...), branch_computations={%region_8.9_spmd, %region_9.10_spmd, %region_10.11_spmd, %region_1... | conditional | bytes 1179696 | solution.py:107
  20.3 4.9 %collective-permute-start.10 = (bf16[2,24,2048]{2,1,0:T(8,128)(2,1)S(1)}, bf16[2,24,2048]{2,1,0:T(8,128)(2,1)S(1)}, u32[]{:S(2)}, u32[]{:S(2)}) collective-permute-start(bf16[2,24,2048]{2,1,0:T(8,128)(2,1)S(1)} %param.12), channel_id=1, source_target_pairs={{0,16},{4,20},{8,24},{12,28},{16,0},{20,4},{24,8},{28,12},{32,48},... | collective-permute-start | bytes 589832 | tf_op jit(solution)/shard_map/cond/branch_4_fun/ppermute | solution.py:102
  25.1 11.0 %collective-permute-done.10 = bf16[2,24,2048]{2,1,0:T(8,128)(2,1)S(1)} collective-permute-done((bf16[2,24,2048]{2,1,0:T(8,128)(2,1)S(1)}, bf16[2,24,2048]{2,1,0:T(8,128)(2,1)S(1)}, u32[]{:S(2)}, u32[]{:S(2)}) %collective-permute-start.10) | collective-permute-done | bytes 196640 | tf_op jit(solution)/shard_map/cond/branch_4_fun/ppermute | solution.py:102
  36.2 0.0 copy-start
  36.2 0.0 copy-start.1
  36.2 8.1 %all-gather.far_ref = bf16[8,24,2048]{2,1,0:T(8,128)(2,1)S(1)} all-gather(bf16[2,24,2048]{2,1,0:T(8,128)(2,1)S(1)} %get-tuple-element.58), channel_id=2, replica_groups=mesh['blk'=128,'pair'=4] {'pair'}, dimensions={0}, use_global_device_ids=true | all-gather | bytes 983040 | tf_op jit(solution)/shard_map/all_gather | solution.py:120
  44.3 0.0 copy-done
  44.3 0.0 copy-done.1
  44.3 27.8 %shard_map.46 = f32[8,2048]{1,0:T(8,128)} custom-call(f32[16]{0:T(128)S(1)} %copy-done.1, bf16[16,2048]{1,0:T(8,128)(2,1)S(1)} %copy-done, bf16[8,24,2048]{2,1,0:T(8,128)(2,1)S(1)} %all-gather.far_ref), custom_call_target="tpu_custom_call" | custom-call | tf_op jit(solution)/shard_map/pallas_call | solution.py:89
  (4 shorter events, 0.1 us)
Async XLA Ops:
  0.0 0.9 %copy-start.2 = (bf16[8,2048]{1,0:T(8,128)(2,1)S(1)}, bf16[8,2048]{1,0:T(8,128)(2,1)}, u32[]{:S(2)}) copy-start(bf16[8,2048]{1,0:T(8,128)(2,1)} %param.29) | copy-start | bytes 98308
  0.9 11.3 %collective-permute-start.22 = (bf16[24,2048]{1,0:T(8,128)(2,1)S(1)}, bf16[24,2048]{1,0:T(8,128)(2,1)S(1)}, u32[]{:S(2)}, u32[]{:S(2)}) collective-permute-start(bf16[24,2048]{1,0:T(8,128)(2,1)S(1)} %constant_dynamic-update-slice_fusion), channel_id=1, source_target_pairs={{0,1},{1,0},{2,3},{3,2},{4,5},{5,4},{6,7},{7,6},{8,9},{9,8},{10,11... | collective-permute-start | bytes 294920 | tf_op jit(solution)/shard_map/ppermute | solution.py:116
  9.7 0.7 copy-start.3
  12.3 7.9 %collective-permute-start.1 = (bf16[2,24,2048]{2,1,0:T(8,128)(2,1)S(1)}, bf16[2,24,2048]{2,1,0:T(8,128)(2,1)S(1)}, u32[]{:S(2)}, u32[]{:S(2)}) collective-permute-start(bf16[2,24,2048]{2,1,0:T(8,128)(2,1)S(1)} %param.2), channel_id=1, source_target_pairs={{0,128},{4,132},{8,136},{12,140},{16,144},{20,148},{24,152},{28,15... | collective-permute-start | bytes 589832 | tf_op jit(solution)/shard_map/cond/branch_2_fun/ppermute | solution.py:102
  20.3 15.9 %collective-permute-start.10 = (bf16[2,24,2048]{2,1,0:T(8,128)(2,1)S(1)}, bf16[2,24,2048]{2,1,0:T(8,128)(2,1)S(1)}, u32[]{:S(2)}, u32[]{:S(2)}) collective-permute-start(bf16[2,24,2048]{2,1,0:T(8,128)(2,1)S(1)} %param.12), channel_id=1, source_target_pairs={{0,16},{4,20},{8,24},{12,28},{16,0},{20,4},{24,8},{28,12},{32,48},... | collective-permute-start | bytes 589832 | tf_op jit(solution)/shard_map/cond/branch_4_fun/ppermute | solution.py:102
  36.2 8.1 %copy-start = (bf16[16,2048]{1,0:T(8,128)(2,1)S(1)}, bf16[16,2048]{1,0:T(8,128)(2,1)}, u32[]{:S(2)}) copy-start(bf16[16,2048]{1,0:T(8,128)(2,1)} %own_ref.1) | copy-start | bytes 196612
  36.2 8.1 %copy-start.1 = (f32[16]{0:T(128)S(1)}, f32[16]{0:T(128)}, u32[]{:S(2)}) copy-start(f32[16]{0:T(128)} %scales.1) | copy-start | bytes 196

commit v4 on v3

--- a/solution.py
+++ b/solution.py
@@ -58,42 +58,57 @@
     return total
 
 
-def product_kernel(scales, own_ref, far_ref, out_ref, own_side, side_a, rows_a, side_b, rows_b):
-    units = far_ref.shape[0]
+def product_kernel(far_count, chained, *refs):
+    scales, own_ref = refs[:2]
+    far_refs = refs[2 : 2 + far_count]
+    rest = refs[2 + far_count :]
+    before, rest = (rest[0], rest[1:]) if chained else (None, rest)
+    out_ref, own_side, side_a, rows_a, side_b, rows_b = rest
     feature = lax.broadcasted_iota(jnp.int32, (16, 1), 0)
     scale = jnp.ones((16, 1), jnp.float32)
     for i in range(16):
         scale = jnp.where(feature == i, scales[i], scale)
     inv_sq = 1.0 / (scale * scale)
     own_side[...] = own_rows(own_ref[...], inv_sq)
-    out_ref[...] = jnp.zeros_like(out_ref)
-    far_prepare(far_ref[0, 0:16, :], inv_sq, side_a, rows_a)
+    units = [(ref, i) for ref in far_refs for i in range(ref.shape[0])]
+    slots = [(side_a, rows_a), (side_b, rows_b)]
 
-    def two_units(pair, carry):
-        first = 2 * pair
-        far_prepare(far_ref[first + 1, 0:16, :], inv_sq, side_b, rows_b)
-        total = add_unit(out_ref[...], rows_a, own_side, far_ref[first, 16:24, :])
-        later = lax.rem(first + 2, units)
-        far_prepare(far_ref[later, 0:16, :], inv_sq, side_a, rows_a)
-        out_ref[...] = add_unit(total, rows_b, own_side, far_ref[first + 1, 16:24, :])
-        return carry
+    def prepare(index):
+        ref, i = units[index]
+        far_prepare(ref[i, 0:16, :], inv_sq, *slots[index % 2])
 
-    lax.fori_loop(0, units // 2, two_units, 0)
+    total = before[...] if chained else jnp.zeros(out_ref.shape, jnp.float32)
+    prepare(0)
+    for index, (ref, i) in enumerate(units):
+        if index + 1 < len(units):
+            prepare(index + 1)
+        total = add_unit(total, slots[index % 2][1], own_side, ref[i, 16:24, :])
+    out_ref[...] = total
 
 
-def block_product(own, scales, far):
+def block_product(own, scales, far, before=None):
     count = own.shape[1]
     side = pltpu.VMEM((DEPTH, count), jnp.bfloat16)
     rows = pltpu.VMEM((count, DEPTH), jnp.bfloat16)
     in_vmem = pl.BlockSpec(memory_space=pltpu.VMEM)
+    chained = before is not None
+    operands = [scales, own, *far] + ([before] if chained else [])
+    entries = sum(part.shape[0] for part in far) * count * count
     return pl.pallas_call(
-        product_kernel,
+        functools.partial(product_kernel, len(far), chained),
         out_shape=jax.ShapeDtypeStruct((8, count), jnp.float32),
-        in_specs=[pl.BlockSpec(memory_space=pltpu.SMEM), in_vmem, in_vmem],
+        in_specs=[pl.BlockSpec(memory_space=pltpu.SMEM)] + [in_vmem] * (len(operands) - 1),
         out_specs=in_vmem,
         scratch_shapes=[side, side, rows, side, rows],
-        compiler_params=pltpu.CompilerParams(vmem_limit_bytes=48 << 20),
-    )(scales, own, far)
+        cost_estimate=pl.CostEstimate(
+            flops=2 * entries * (DEPTH + 8), bytes_accessed=1 << 20, transcendentals=entries
+        ),
+        compiler_params=pltpu.CompilerParams(vmem_limit_bytes=32 << 20),
+    )(*operands)
+
+
+def swap(shard, offset):
+    return lax.ppermute(shard, "pair", [(i, i ^ offset) for i in range(lax.axis_size("pair"))])
 
 
 def move(mask, shard):
@@ -113,12 +128,15 @@
     round_index = jnp.bitwise_and(lax.axis_index("pair"), 1)
     mask = jnp.bitwise_xor(jnp.where(round_index == 0, partners[0, 0], partners[1, 0]), lax.axis_index("blk"))
     mine = jnp.concatenate([points, values], 0)
-    sibling = lax.ppermute(mine, "pair", [(i, i ^ 1) for i in range(lax.axis_size("pair"))])
-    far = jnp.stack([mine, sibling])
+    far = jnp.stack([mine, swap(mine, 1)])
     far = hop(far, mask, bits - near, near)
     far = hop(far, mask, 0, bits - near)
-    far = lax.all_gather(far, "pair", axis=0)
-    return block_product(points, length_scales, far.reshape((-1,) + mine.shape))
+    second = swap(far, 2)
+    product = block_product(points, length_scales, [far])
+    second, product = lax.optimization_barrier((second, product))
+    others = swap(jnp.concatenate([far, second]), 1)
+    product = block_product(points, length_scales, [second], product)
+    return block_product(points, length_scales, [others], product)
 
 
 def solution(mesh):

time: 72.6 us -> 77.3 us (1.065)
  starting transfers between devices: 15.6 us -> 38.9 us
  waiting for transfers between devices: 17 us -> 5.34 us
  blocking collectives: 8.11 us -> 0 us
  Pallas kernels: 27.8 us -> 28.9 us
    ppermute x1 -> x3, starting transfers between devices: 8.79 us -> 28.8 us  [swap(): lax.ppermute(shard, 'pair', [(i, i ^ offset) for i in range(lax.axis_size...]
    ppermute x2 -> x1, waiting for transfers between devices: 17 us -> 5.34 us  [move(): lax.ppermute(shard, 'blk', [(i, i ^ mask) for i in range(lax.axis_size('b...]
    all_gather x1 -> x0, blocking collectives: 8.11 us -> none  [shards(): far = lax.all_gather(far, 'pair', axis=0)]
    ppermute x2 -> x1, starting transfers between devices: 6.8 us -> 10.1 us  [move(): lax.ppermute(shard, 'blk', [(i, i ^ mask) for i in range(lax.axis_size('b...]
    pallas_call x1 -> x3, Pallas kernels: 27.8 us -> 28.9 us  [block_product(): pl.pallas_call(functools.partial(product_kernel, len(far), chained), out_...]
  transfers between devices with their start and end apart: 3 -> 4, of which waited for: 2 -> 1; matrix products, arithmetic and copies ran while one was open for 1% -> 1% of each run, Pallas kernels for 0% -> 19%
where the time goes in v4:
time: 77.3 us; the launch traced here: 76.8 us
  starting transfers between devices  38.9 us (50%)
  Pallas kernels  28.9 us (37%)
  waiting for transfers between devices  5.34 us (7%)
  local copies, waits for them, and re-layouts  2.13 us (3%)
  between operations  1.47 us (2%)
    pallas_call x3, Pallas kernels, block_product(): pl.pallas_call(functools.partial(product_kernel, len(far), chained), out_...  28.9 us
    ppermute x3, starting transfers between devices, swap(): lax.ppermute(shard, 'pair', [(i, i ^ offset) for i in range(lax.axis_size...  28.8 us
    ppermute x1, starting transfers between devices, move(): lax.ppermute(shard, 'blk', [(i, i ^ mask) for i in range(lax.axis_size('b...  10.1 us
    ppermute x1, waiting for transfers between devices, move(): lax.ppermute(shard, 'blk', [(i, i ^ mask) for i in range(lax.axis_size('b...  5.34 us
  transfers between devices with their start and end apart: 4, of which 1 were waited for; matrix products, arithmetic and copies ran while one was open for 1% of the time, Pallas kernels for 19%

profile of v4, /device:TPU:1, one launch (start us, length us, event | category | flops | bytes accessed | tf_op | source)
XLA Modules:
  0.0 76.8 jit_solution(17876558453786806269)
XLA Ops:
  0.0 0.0 copy-start.2
  0.0 0.9 %constant_dynamic-update-slice_fusion.1 = bf16[24,2048]{1,0:T(8,128)(2,1)S(1)} fusion(bf16[16,2048]{1,0:T(8,128)(2,1)} %refs_1_.5), kind=kLoop, calls=%fused_computation.3 | loop fusion | bytes 131072
  0.9 0.0 copy-done.2
  0.9 8.8 %collective-permute-start.22 = (bf16[24,2048]{1,0:T(8,128)(2,1)S(1)}, bf16[24,2048]{1,0:T(8,128)(2,1)S(1)}, u32[]{:S(2)}, u32[]{:S(2)}) collective-permute-start(bf16[24,2048]{1,0:T(8,128)(2,1)S(1)} %constant_dynamic-update-slice_fusion), channel_id=1, source_target_pairs={{0,1},{1,0},{2,3},{3,2},{4,5},{5,4},{6,7},{7,6},{8,9},{9,8},{10,11... | collective-permute-start | bytes 294920 | tf_op jit(solution)/shard_map/ppermute | solution.py:111
  9.7 0.0 copy-start.3
  9.7 0.6 copy-done.3
  10.3 0.6 fusion
  12.3 0.0 collective-permute-done.22
  12.4 0.0 copy-start
  12.4 15.5 %conditional.3 = (bf16[2,24,2048]{2,1,0:T(8,128)(2,1)S(1)}) conditional(s32[]{:T(128)} %clamp.6, bf16[2,24,2048]{2,1,0:T(8,128)(2,1)S(1)} %get-tuple-element.61, bf16[2,24,2048]{2,1,0:T(8,128)(2,1)S(1)} %get-tuple-element.61, bf16[2,24,2048]{2,1,0:T(8,128)(2,1)S(1)} %get-tuple-element.61, ...), branch_computations={%region_8.9_spmd, %region_9.10_spmd, %region_10.11_spmd, %region_1... | conditional | bytes 1179696 | solution.py:122
  12.4 10.1 %collective-permute-start.14 = (bf16[2,24,2048]{2,1,0:T(8,128)(2,1)S(1)}, bf16[2,24,2048]{2,1,0:T(8,128)(2,1)S(1)}, u32[]{:S(2)}, u32[]{:S(2)}) collective-permute-start(bf16[2,24,2048]{2,1,0:T(8,128)(2,1)S(1)} %param.16), channel_id=1, source_target_pairs={{0,32},{4,36},{8,40},{12,44},{16,48},{20,52},{24,56},{28,60},{32,0... | collective-permute-start | bytes 589832 | tf_op jit(solution)/shard_map/cond/branch_8_fun/ppermute | solution.py:117
  22.5 5.3 %collective-permute-done.14 = bf16[2,24,2048]{2,1,0:T(8,128)(2,1)S(1)} collective-permute-done((bf16[2,24,2048]{2,1,0:T(8,128)(2,1)S(1)}, bf16[2,24,2048]{2,1,0:T(8,128)(2,1)S(1)}, u32[]{:S(2)}, u32[]{:S(2)}) %collective-permute-start.14) | collective-permute-done | bytes 196640 | tf_op jit(solution)/shard_map/cond/branch_8_fun/ppermute | solution.py:117
  27.9 0.0 copy-start.1
  27.9 2.8 %collective-permute-start.23 = (bf16[2,24,2048]{2,1,0:T(8,128)(2,1)S(1)}, bf16[2,24,2048]{2,1,0:T(8,128)(2,1)S(1)}, u32[]{:S(2)}, u32[]{:S(2)}) collective-permute-start(bf16[2,24,2048]{2,1,0:T(8,128)(2,1)S(1)} %get-tuple-element.62.refs_2_), channel_id=1, source_target_pairs={{0,2},{1,3},{2,0},{3,1},{4,6},{5,7},{6,4},{7,5},{8,10},{9,11},{10,... | collective-permute-start | bytes 589832 | tf_op jit(solution)/shard_map/ppermute | solution.py:111
  30.7 0.0 copy-done
  30.7 0.0 copy-done.1
  30.7 7.2 %shard_map.46.refs_3_ = f32[8,2048]{1,0:T(8,128)S(1)} custom-call(f32[16]{0:T(128)S(1)} %copy-done.1, bf16[16,2048]{1,0:T(8,128)(2,1)S(1)} %copy-done, bf16[2,24,2048]{2,1,0:T(8,128)(2,1)S(1)} %get-tuple-element.62.refs_2_), custom_call_target="tpu_custom_call" | custom-call | flops 1207959552 | bytes 1048576 | tf_op jit(solution)/shard_map/pallas_call | solution.py:97
  37.9 0.0 collective-permute-done.23.refs_2_
  38.0 17.2 %collective-permute-start.24 = (bf16[4,24,2048]{2,1,0:T(8,128)(2,1)S(1)}, bf16[4,24,2048]{2,1,0:T(8,128)(2,1)S(1)}, u32[]{:S(2)}, u32[]{:S(2)}) collective-permute-start(bf16[4,24,2048]{2,1,0:T(8,128)(2,1)S(1)} %pad_maximum_fusion), channel_id=1, source_target_pairs={{0,1},{1,0},{2,3},{3,2},{4,5},{5,4},{6,7},{7,6},{8,9},{9,8},{10,11... | collective-permute-start | bytes 1179656 | tf_op jit(solution)/shard_map/ppermute | solution.py:111
  55.2 7.2 %shard_map.47.refs_3_ = f32[8,2048]{1,0:T(8,128)S(1)} custom-call(f32[16]{0:T(128)S(1)} %copy-done.1, bf16[16,2048]{1,0:T(8,128)(2,1)S(1)} %copy-done, bf16[2,24,2048]{2,1,0:T(8,128)(2,1)S(1)} %collective-permute-done.23.refs_2_, f32[8,2048]{1,0:T(8,128)S(1)} %shard_map.46.refs_3_), custom_call_target="tpu_custom_call" | custom-call | flops 1207959552 | bytes 1048576 | tf_op jit(solution)/shard_map/pallas_call | solution.py:97
  62.3 0.0 collective-permute-done.24.refs_2_
  62.3 14.5 %shard_map.48 = f32[8,2048]{1,0:T(8,128)} custom-call(f32[16]{0:T(128)S(1)} %copy-done.1, bf16[16,2048]{1,0:T(8,128)(2,1)S(1)} %copy-done, bf16[4,24,2048]{2,1,0:T(8,128)(2,1)S(1)} %collective-permute-done.24.refs_2_, f32[8,2048]{1,0:T(8,128)S(1)} %shard_map.47.refs_3_), custom_call_target="tpu_custom_call" | custom-call | flops 2415919104 | bytes 1048576 | tf_op jit(solution)/shard_map/pallas_call | solution.py:97
  (5 shorter events, 0.1 us)
Async XLA Ops:
  0.0 0.9 %copy-start.2 = (bf16[8,2048]{1,0:T(8,128)(2,1)S(1)}, bf16[8,2048]{1,0:T(8,128)(2,1)}, u32[]{:S(2)}) copy-start(bf16[8,2048]{1,0:T(8,128)(2,1)} %param.29) | copy-start | bytes 98308
  0.9 11.4 %collective-permute-start.22 = (bf16[24,2048]{1,0:T(8,128)(2,1)S(1)}, bf16[24,2048]{1,0:T(8,128)(2,1)S(1)}, u32[]{:S(2)}, u32[]{:S(2)}) collective-permute-start(bf16[24,2048]{1,0:T(8,128)(2,1)S(1)} %constant_dynamic-update-slice_fusion), channel_id=1, source_target_pairs={{0,1},{1,0},{2,3},{3,2},{4,5},{5,4},{6,7},{7,6},{8,9},{9,8},{10,11... | collective-permute-start | bytes 294920 | tf_op jit(solution)/shard_map/ppermute | solution.py:111
  9.7 0.7 copy-start.3
  12.4 18.4 %copy-start = (bf16[16,2048]{1,0:T(8,128)(2,1)S(1)}, bf16[16,2048]{1,0:T(8,128)(2,1)}, u32[]{:S(2)}) copy-start(bf16[16,2048]{1,0:T(8,128)(2,1)} %refs_1_.5) | copy-start | bytes 196612
  12.4 15.4 %collective-permute-start.14 = (bf16[2,24,2048]{2,1,0:T(8,128)(2,1)S(1)}, bf16[2,24,2048]{2,1,0:T(8,128)(2,1)S(1)}, u32[]{:S(2)}, u32[]{:S(2)}) collective-permute-start(bf16[2,24,2048]{2,1,0:T(8,128)(2,1)S(1)} %param.16), channel_id=1, source_target_pairs={{0,32},{4,36},{8,40},{12,44},{16,48},{20,52},{24,56},{28,60},{32,0... | collective-permute-start | bytes 589832 | tf_op jit(solution)/shard_map/cond/branch_8_fun/ppermute | solution.py:117
  27.9 2.9 %copy-start.1 = (f32[16]{0:T(128)S(1)}, f32[16]{0:T(128)}, u32[]{:S(2)}) copy-start(f32[16]{0:T(128)} %refs_0_.5) | copy-start | bytes 196
  27.9 10.1 %collective-permute-start.23 = (bf16[2,24,2048]{2,1,0:T(8,128)(2,1)S(1)}, bf16[2,24,2048]{2,1,0:T(8,128)(2,1)S(1)}, u32[]{:S(2)}, u32[]{:S(2)}) collective-permute-start(bf16[2,24,2048]{2,1,0:T(8,128)(2,1)S(1)} %get-tuple-element.62.refs_2_), channel_id=1, source_target_pairs={{0,2},{1,3},{2,0},{3,1},{4,6},{5,7},{6,4},{7,5},{8,10},{9,11},{10,... | collective-permute-start | bytes 589832 | tf_op jit(solution)/shard_map/ppermute | solution.py:111
  38.0 24.4 %collective-permute-start.24 = (bf16[4,24,2048]{2,1,0:T(8,128)(2,1)S(1)}, bf16[4,24,2048]{2,1,0:T(8,128)(2,1)S(1)}, u32[]{:S(2)}, u32[]{:S(2)}) collective-permute-start(bf16[4,24,2048]{2,1,0:T(8,128)(2,1)S(1)} %pad_maximum_fusion), channel_id=1, source_target_pairs={{0,1},{1,0},{2,3},{3,2},{4,5},{5,4},{6,7},{7,6},{8,9},{9,8},{10,11... | collective-permute-start | bytes 1179656 | tf_op jit(solution)/shard_map/ppermute | solution.py:111
